TPU v7x, 512 devices: a whole 4x8x8 slice. The times are simulated.
512 devices in a mesh: lat: 32 (over z_lo, y), lon: 16 (over x, z_hi, core).
Axes of the slice: x: 4, y: 8, z: 8 (z_hi: 2, z_lo: 4; z = z_hi * 4 + z_lo), core: 2. Of those that a mesh axis runs over, the one named last changes fastest.
Arguments:
- activations: bfloat16 [128, 512, 256], P('lat', 'lon'), may hold values from -23 to 23
- basis_weights: bfloat16 [9, 128, 7, 7], replicated, may hold values from -0.875 to 0.875
- extents: int32 [2, 128, 7], replicated, may hold values from 0 to 3
- mix_weight: bfloat16 [9, 16, 16, 16], replicated, may hold values from -0.5 to 0.5
- spec_filter: float32 [2, 256, 128], P(None, 'lon'), may hold values from -6 to 6
- w_in: bfloat16 [256, 512], replicated, may hold values from -0.375 to 0.375
- w_out: bfloat16 [512, 256], replicated, may hold values from -0.25 to 0.25
- cotangent: bfloat16 [128, 512, 256], P('lat', 'lon'), may hold values from -6 to 6
Outputs:
- block_output: bfloat16 [128, 512, 256], P('lat', 'lon')
- grad_x: bfloat16 [128, 512, 256], P('lat', 'lon')
- grad_filter: float32 [2, 256, 128], P(None, 'lon')
All inputs are finite; a program needn't handle non-finite values.
Results may differ from a plain program's by a relative error of at most 0.02.
Values may be sent and summed in bfloat16 or wider, within the bound.
A program may use at most 128 MiB of HBM per device.

v0:
```python
import math

import jax
import jax.numpy as jnp
import numpy as np
from jax import lax
from jax.sharding import PartitionSpec as P

HIGHEST = lax.Precision.HIGHEST
EPSILON = 1e-05


def padded(value, sides, width):
    for axis, dim in sides:
        count, length = (lax.axis_size(axis), value.shape[dim])
        up = [(i, (i + 1) % count) for i in range(count)]
        down = [(j, i) for i, j in up]
        last = lax.slice_in_dim(value, length - width, length, axis=dim)
        initial = lax.slice_in_dim(value, 0, width, axis=dim)
        before = lax.ppermute(last, axis, up)
        after = lax.ppermute(initial, axis, down)
        value = jnp.concatenate([before, value, after], axis=dim)
    return value


def layer_norm(values):
    centred = values - jnp.mean(values, axis=-1, keepdims=True)
    inverse = lax.rsqrt(jnp.mean(centred * centred, axis=-1, keepdims=True) + EPSILON)
    return (centred * inverse, inverse)


def norm_back(normed, inverse, upstream):
    return inverse * (
        upstream
        - jnp.mean(upstream, axis=-1, keepdims=True)
        - normed * jnp.mean(upstream * normed, axis=-1, keepdims=True)
    )


def gelu_slope(values):
    return 0.5 * (1.0 + jax.scipy.special.erf(values * (1.0 / math.sqrt(2.0)))) + values * jnp.exp(
        -0.5 * values * values
    ) * (1.0 / math.sqrt(2.0 * math.pi))


def quad_weights(lat_total):
    theta = math.pi * (jnp.arange(lat_total, dtype=jnp.float32) + 0.5) / lat_total
    return math.pi / lat_total * jnp.sin(theta)


def legendre_table(orders, lat_total, degree_total, order_total):
    theta = math.pi * (jnp.arange(lat_total, dtype=jnp.float32) + 0.5) / lat_total
    cosine = jnp.cos(theta)
    log_sine = jnp.log(jnp.sin(theta))
    counter = jnp.arange(1, order_total, dtype=jnp.int32).astype(jnp.float32)
    growth = jnp.concatenate(
        [
            jnp.zeros((1,), jnp.float32),
            jnp.cumsum(0.5 * jnp.log((2.0 * counter + 1.0) / (2.0 * counter))),
        ]
    )
    order_float = orders.astype(jnp.float32)
    diagonal = jnp.exp(
        -0.5 * math.log(4.0 * math.pi)
        + jnp.take(growth, orders)[:, None]
        + order_float[:, None] * log_sine[None, :]
    )

    def advance(carry, degree):
        latest, earlier = carry
        degree_float = degree.astype(jnp.float32)
        upper = jnp.sqrt(
            jnp.maximum(4.0 * degree_float * degree_float - 1.0, 1.0)
            / jnp.maximum(degree_float * degree_float - order_float * order_float, 1.0)
        )
        below = degree_float - 1.0
        lower_coef = jnp.sqrt(
            jnp.maximum(below * below - order_float * order_float, 0.0)
            / jnp.maximum(4.0 * below * below - 1.0, 1.0)
        )
        recurred = upper[:, None] * (cosine[None, :] * latest - lower_coef[:, None] * earlier)
        value = jnp.where(
            degree < orders[:, None],
            jnp.zeros_like(recurred),
            jnp.where(degree == orders[:, None], diagonal, recurred),
        )
        return ((value, latest), value)

    zeros = jnp.zeros((orders.shape[0], lat_total), jnp.float32)
    final, table = lax.scan(
        advance, (zeros, zeros), jnp.arange(degree_total, dtype=jnp.int32), unroll=8
    )
    return table


def fourier_tables(order_list, lon_total):
    positions = jnp.arange(lon_total, dtype=jnp.int32)
    phase_index = positions[:, None] * order_list[None, :] % lon_total
    angle = phase_index.astype(jnp.float32) * (2.0 * math.pi / lon_total)
    paired_trig = jnp.stack([jnp.cos(angle), -jnp.sin(angle)], axis=-1)
    order_weight = jnp.where(order_list == 0, 1.0, 2.0).astype(jnp.float32)
    analysis = (paired_trig * (2.0 * math.pi / lon_total)).reshape(lon_total, -1)
    synthesis = (paired_trig * order_weight[None, :, None]).reshape(lon_total, -1)
    return (analysis, synthesis)


def keep_taps(weights, extents):
    tap_total = weights.shape[-1]
    shift = jnp.arange(tap_total, dtype=jnp.int32) - (tap_total - 1) // 2
    inside = (shift >= -extents[0][..., None]) & (shift <= extents[1][..., None])
    return jnp.where(inside, weights, jnp.zeros_like(weights))


def block_dense(mix_weight):
    basis_count, group_count, group_size, unused = mix_weight.shape
    diagonal_ones = jnp.eye(group_count, dtype=mix_weight.dtype)
    expanded = mix_weight[:, :, :, None, :] * diagonal_ones[None, :, None, :, None]
    return expanded.reshape(basis_count, group_count * group_size, group_count * group_size)


def band_matrix(kept, width_out, width_in, offset):
    tap_total = kept.shape[-1]
    out_pos = jnp.arange(width_out, dtype=jnp.int32)[:, None, None]
    in_pos = jnp.arange(width_in, dtype=jnp.int32)[None, :, None]
    tap_pos = jnp.arange(tap_total, dtype=jnp.int32)[None, None, :]
    picker = (in_pos + offset == out_pos + tap_pos).astype(jnp.bfloat16)
    return jnp.einsum("lrd,njd->lrnj", kept, picker, preferred_element_type=jnp.float32).astype(
        jnp.bfloat16
    )


def widen(field, first_row, lat_total, reach):
    wide = padded(field, (("lat", 0), ("lon", 1)), reach)
    global_rows = first_row - reach + jnp.arange(wide.shape[0], dtype=jnp.int32)
    inside = (global_rows >= 0) & (global_rows < lat_total)
    return jnp.where(inside[:, None, None], wide, jnp.zeros_like(wide))


def to_channels(field):
    return lax.all_to_all(field, "lon", split_axis=2, concat_axis=1, tiled=True)


def to_orders(field):
    return lax.all_to_all(
        field.astype(jnp.bfloat16), "lat", split_axis=0, concat_axis=2, tiled=True
    ).astype(field.dtype)


def to_latitudes(field):
    return lax.all_to_all(
        field.astype(jnp.bfloat16), "lat", split_axis=1, concat_axis=0, tiled=True
    ).astype(field.dtype)


def to_longitudes(field):
    return lax.all_to_all(
        field.astype(jnp.bfloat16), "lon", split_axis=1, concat_axis=2, tiled=True
    ).astype(field.dtype)


def analyse(field, legendre, own_orders, order_spans, block_len):
    degree_total = legendre.shape[0]
    block_total = degree_total // block_len
    results = []
    for span_low, span_high in order_spans:
        table = legendre
        section = field
        first_block = jnp.min(own_orders) // block_len

        def analyse_step(block, accum, table=table, section=section):
            value = jnp.einsum("lmt,mrct->mcrl", table, section, precision=HIGHEST)
            return value

        initial = jnp.zeros((span_high - span_low, field.shape[2], 2, degree_total), jnp.float32)
        results.append(lax.fori_loop(first_block, block_total, analyse_step, initial))
    return results[0]


def synthesise(coefs, legendre, own_orders, order_spans, block_len):
    degree_total = legendre.shape[0]
    lat_total = legendre.shape[2]
    block_total = degree_total // block_len
    results = []
    for span_low, span_high in order_spans:
        table = legendre
        section = coefs
        first_block = jnp.min(own_orders) // block_len

        def synthesise_step(block, accum, table=table, section=section):
            return accum + jnp.einsum("lmt,mcrl->mrtc", table, section, precision=HIGHEST)

        initial = jnp.zeros((span_high - span_low, 2, lat_total, coefs.shape[1]), jnp.float32)
        results.append(lax.fori_loop(first_block, block_total, synthesise_step, initial))
    return results[0]


def local(activations, basis_weights, extents, mix_weight, spec_filter, w_in, w_out, cotangent):
    lat_rows, lon_cols, channels = activations.shape
    basis_count = basis_weights.shape[0]
    lat_total = basis_weights.shape[1]
    tap_count = basis_weights.shape[2]
    reach = (tap_count - 1) // 2
    lat_devices = lax.axis_size("lat")
    lon_total = lon_cols * lax.axis_size("lon")
    part_chans = channels // lax.axis_size("lon")
    orders_dev = lat_total // lat_devices
    block_len = min(128, lat_total)
    lat_index = lax.axis_index("lat")
    row_start = lat_index * lat_rows
    order_list = np.arange(lat_total)
    order_spans = ((0, orders_dev),)
    order_list = jnp.asarray(order_list, dtype=jnp.int32)
    own_orders = lax.dynamic_slice_in_dim(order_list, lat_index * orders_dev, orders_dev)
    legendre = legendre_table(own_orders, lat_total, lat_total, lat_total)
    quadrature = quad_weights(lat_total)
    analysis, synthesis = fourier_tables(order_list, lon_total)
    dense_mix = block_dense(mix_weight)
    source = activations.astype(jnp.float32)
    normed_in, inverse_in = layer_norm(source)
    wide_in = widen(normed_in.astype(jnp.bfloat16), row_start, lat_total, reach)
    kept_own = keep_taps(
        lax.dynamic_slice_in_dim(basis_weights, row_start, lat_rows, 1),
        lax.dynamic_slice_in_dim(extents, row_start, lat_rows, 1),
    )
    windows = jnp.stack(
        [wide_in[offset : offset + lat_rows] for offset in range(tap_count)], axis=1
    )
    mix_total = jnp.zeros((lat_rows, lon_cols, channels), jnp.float32)
    for basis_index in range(basis_count):
        banded = band_matrix(kept_own[basis_index], lon_cols, lon_cols + 2 * reach, 0)
        filtered = lax.dot_general(
            banded, windows, (((1, 3), (1, 2)), ((0,), (0,))), preferred_element_type=jnp.float32
        ).astype(jnp.bfloat16)
        mix_total = mix_total + jnp.einsum(
            "lni,io->lno", filtered, dense_mix[basis_index], preferred_element_type=jnp.float32
        )
    mixed_in = mix_total.astype(jnp.bfloat16)
    fourier = jnp.einsum(
        "anc,nk->kca", to_channels(mixed_in).astype(jnp.float32), analysis, precision=HIGHEST
    )
    by_order = (
        to_orders(fourier).reshape(orders_dev, 2, part_chans, lat_total)
        * quadrature[None, None, None, :]
    )
    coefficient = analyse(by_order, legendre, own_orders, order_spans, block_len)
    filter_real = spec_filter[0][None]
    filter_imag = spec_filter[1][None]
    product = jnp.stack(
        [
            coefficient[:, :, 0] * filter_real - coefficient[:, :, 1] * filter_imag,
            coefficient[:, :, 0] * filter_imag + coefficient[:, :, 1] * filter_real,
        ],
        axis=2,
    )
    synthesized = synthesise(product, legendre, own_orders, order_spans, block_len).reshape(
        2 * orders_dev, lat_total, part_chans
    )
    spectral = to_longitudes(
        jnp.einsum("kac,nk->anc", to_latitudes(synthesized), synthesis, precision=HIGHEST)
    )
    carried = source + spectral
    normed_mid, inverse_mid = layer_norm(carried)
    middle = normed_mid.astype(jnp.bfloat16)
    preact = jnp.einsum("anc,ch->anh", middle, w_in, preferred_element_type=jnp.float32)
    hidden = jax.nn.gelu(preact, approximate=False).astype(jnp.bfloat16)
    block_output = (
        carried + jnp.einsum("anh,hc->anc", hidden, w_out, preferred_element_type=jnp.float32)
    ).astype(jnp.bfloat16)
    d_hidden = jnp.einsum("anc,hc->anh", cotangent, w_out, preferred_element_type=jnp.float32)
    d_preact = (d_hidden * gelu_slope(preact)).astype(jnp.bfloat16)
    d_normed = jnp.einsum("anh,ch->anc", d_preact, w_in, preferred_element_type=jnp.float32)
    d_carried = cotangent.astype(jnp.float32) + norm_back(normed_mid, inverse_mid, d_normed)
    d_spec = d_carried.astype(jnp.bfloat16)
    d_synth = jnp.einsum(
        "anc,nk->kca", to_channels(d_spec).astype(jnp.float32), synthesis, precision=HIGHEST
    )
    d_by_order = to_orders(d_synth).reshape(orders_dev, 2, part_chans, lat_total)
    d_product = analyse(d_by_order, legendre, own_orders, order_spans, block_len)
    grad_real = jnp.sum(
        d_product[:, :, 0] * coefficient[:, :, 0] + d_product[:, :, 1] * coefficient[:, :, 1],
        axis=0,
    )
    grad_imag = jnp.sum(
        d_product[:, :, 1] * coefficient[:, :, 0] - d_product[:, :, 0] * coefficient[:, :, 1],
        axis=0,
    )
    grad_filter = lax.psum(jnp.stack([grad_real, grad_imag]), "lat")
    d_coeff = jnp.stack(
        [
            d_product[:, :, 0] * filter_real + d_product[:, :, 1] * filter_imag,
            d_product[:, :, 1] * filter_real - d_product[:, :, 0] * filter_imag,
        ],
        axis=2,
    )
    d_fourier = (
        synthesise(d_coeff, legendre, own_orders, order_spans, block_len)
        * quadrature[None, None, :, None]
    ).reshape(2 * orders_dev, lat_total, part_chans)
    d_mixed = to_longitudes(
        jnp.einsum("kac,nk->anc", to_latitudes(d_fourier), analysis, precision=HIGHEST)
    ).astype(jnp.bfloat16)
    wide_grad = widen(d_mixed, row_start, lat_total, reach)
    tap_index = jnp.arange(tap_count, dtype=jnp.int32)[None, :]
    source_rows = row_start + reach + jnp.arange(lat_rows, dtype=jnp.int32)[:, None] - tap_index
    clipped = jnp.clip(source_rows, 0, lat_total - 1)
    kept_back = keep_taps(basis_weights[:, clipped, tap_index], extents[:, clipped, tap_index])
    wide_cols = lon_cols + 2 * reach
    d_normed_in = jnp.zeros((lat_rows, lon_cols, channels), jnp.float32)
    for basis_index in range(basis_count):
        d_filtered = jnp.einsum(
            "lno,io->lni", wide_grad, dense_mix[basis_index], preferred_element_type=jnp.float32
        ).astype(jnp.bfloat16)
        back_windows = jnp.stack(
            [
                d_filtered[2 * reach - offset : 2 * reach - offset + lat_rows]
                for offset in range(tap_count)
            ],
            axis=1,
        )
        banded = band_matrix(kept_back[basis_index], wide_cols, lon_cols, 2 * reach)
        d_normed_in = d_normed_in + lax.dot_general(
            banded,
            back_windows,
            (((1, 2), (1, 2)), ((0,), (0,))),
            preferred_element_type=jnp.float32,
        )
    grad_x = (d_carried + norm_back(normed_in, inverse_in, d_normed_in)).astype(jnp.bfloat16)
    return (block_output, grad_x, grad_filter)


def solution(mesh):
    placed = (
        P("lat", "lon", None),
        P(),
        P(),
        P(),
        P(None, "lon", None),
        P(),
        P(),
        P("lat", "lon", None),
    )
    return jax.shard_map(
        local,
        mesh=mesh,
        in_specs=placed,
        out_specs=(P("lat", "lon", None), P("lat", "lon", None), P(None, "lon", None)),
        check_vma=False,
    )
```

profile of v0, /device:TPU:2, one launch (start us, length us, event | category | flops | bytes accessed | tf_op | source)
XLA Modules:
  0.0 770.4 jit_solution(16966520270048657274)
XLA Ops:
  7.8 9.2 %collective-permute-start.1 = (bf16[3,32,256]{2,1,0:T(8,128)(2,1)}, bf16[3,32,256]{2,1,0:T(8,128)(2,1)}, u32[]{:S(2)}, u32[]{:S(2)}) collective-permute-start(bf16[3,32,256]{2,1,0:T(8,128)(2,1)} %get-tuple-element.595), channel_id=1, source_target_pairs={{16,0},{32,16},{48,32},{64,48},{80,64},{96,80},{112,96},{128,112},... | collective-permute-start | bytes 147464 | tf_op jit(solution)/shard_map/ppermute | solution.py:21
  48.4 6.4 fusion.300
  60.8 322.2 %while.71 = (s32[]{:T(128)}, f32[4,128]{1,0:T(4,128)S(1)}, f32[4,128]{1,0:T(4,128)S(1)}, f32[16,8,4,128]{3,2,1,0:T(4,128)}, s32[16,8]{0,1:T(8,128)S(1)}, /*index...) while((s32[]{:T(128)}, f32[4,128]{1,0:T(4,128)S(1)}, ...), condition=%wide.region_5.6_spmd.clone.clone, body=%wide.region_4.5_spmd.clone.clone.sunk | while | flops 34914 | bytes 118460 | solution.py:90
  67.8 6.3 broadcast_compare_fusion.17
  88.0 6.3 broadcast_compare_fusion.17
  108.1 6.3 broadcast_compare_fusion.17
  128.2 6.3 broadcast_compare_fusion.17
  148.4 6.3 broadcast_compare_fusion.17
  168.5 6.3 broadcast_compare_fusion.17
  188.7 6.3 broadcast_compare_fusion.17
  208.8 6.3 broadcast_compare_fusion.17
  390.1 8.6 %collective-permute-start.3 = (bf16[10,3,256]{2,1,0:T(4,128)(2,1)}, bf16[10,3,256]{2,1,0:T(4,128)(2,1)S(1)}, u32[]{:S(2)}, u32[]{:S(2)}) collective-permute-start(bf16[10,3,256]{2,1,0:T(4,128)(2,1)} %get-tuple-element.587), channel_id=1, source_target_pairs={{1,0},{2,1},{3,2},{4,3},{5,4},{6,5},{7,6},{8,7},{9,8},{10,9},{11,1... | collective-permute-start | bytes 46088 | tf_op jit(solution)/shard_map/ppermute | solution.py:21
  440.6 9.7 %all-to-all-start = ((bf16[16,2,1024]{2,1,0:T(2,128)(2,1)}), bf16[16,2,1024]{2,1,0:T(2,128)(2,1)S(1)}, u32[]{:S(2)}, u32[]{:S(2)}) async-start(bf16[16,2,1024]{2,1,0:T(2,128)(2,1)} %reshape.958), calls=%async_computation | async-start | bytes 131072 | tf_op jit(solution)/shard_map/all_to_all | solution.py:140
  451.1 7.9 %all-to-all-done = bf16[16,2,1024]{2,1,0:T(2,128)(2,1)S(1)} async-done(((bf16[16,2,1024]{2,1,0:T(2,128)(2,1)}), bf16[16,2,1024]{2,1,0:T(2,128)(2,1)S(1)}, u32[]{:S(2)}, u32[]{:S(2)}) %all-to-all-start) | async-done | bytes 65568 | tf_op jit(solution)/shard_map/all_to_all | solution.py:140
  461.0 7.2 all-to-all-start.1
  468.3 10.1 %all-to-all-done.1 = bf16[32,2,256]{2,1,0:T(2,128)(2,1)S(1)} async-done(((bf16[32,2,256]{2,1,0:T(2,128)(2,1)}), bf16[32,2,256]{2,1,0:T(2,128)(2,1)S(1)}, u32[]{:S(2)}, u32[]{:S(2)}) %all-to-all-start.1) | async-done | bytes 32800 | tf_op jit(solution)/shard_map/all_to_all | solution.py:144
  490.4 7.9 %all-to-all-done.2 = bf16[32,2,256]{2,1,0:T(2,128)(2,1)S(1)} async-done(((bf16[32,2,256]{2,1,0:T(2,128)(2,1)}), bf16[32,2,256]{2,1,0:T(2,128)(2,1)S(1)}, u32[]{:S(2)}, u32[]{:S(2)}) %all-to-all-start.2) | async-done | bytes 32800 | tf_op jit(solution)/shard_map/all_to_all | solution.py:150
  507.1 7.0 all-to-all-done.3
  526.4 7.0 all-to-all-done.4
  541.0 8.5 %all-to-all-done.5 = bf16[32,2,256]{2,1,0:T(2,128)(2,1)S(1)} async-done(((bf16[32,2,256]{2,1,0:T(2,128)(2,1)}), bf16[32,2,256]{2,1,0:T(2,128)(2,1)S(1)}, u32[]{:S(2)}, u32[]{:S(2)}) %all-to-all-start.5) | async-done | bytes 32800 | tf_op jit(solution)/shard_map/all_to_all | solution.py:144
  559.4 8.5 %all-to-all-done.6 = bf16[32,2,256]{2,1,0:T(2,128)(2,1)S(1)} async-done(((bf16[32,2,256]{2,1,0:T(2,128)(2,1)}), bf16[32,2,256]{2,1,0:T(2,128)(2,1)S(1)}, u32[]{:S(2)}, u32[]{:S(2)}) %all-to-all-start.6) | async-done | bytes 32800 | tf_op jit(solution)/shard_map/all_to_all | solution.py:150
  589.9 7.2 collective-permute-start.5
  600.7 8.4 %collective-permute-start.7 = (bf16[10,3,256]{2,1,0:T(4,128)(2,1)S(1)}, bf16[10,3,256]{2,1,0:T(4,128)(2,1)S(1)}, u32[]{:S(2)}, u32[]{:S(2)}) collective-permute-start(bf16[10,3,256]{2,1,0:T(4,128)(2,1)S(1)} %get-tuple-element.585), channel_id=1, source_target_pairs={{1,0},{2,1},{3,2},{4,3},{5,4},{6,5},{7,6},{8,7},{9,8},{10,9},{11,1... | collective-permute-start | bytes 46088 | tf_op jit(solution)/shard_map/ppermute | solution.py:21
  609.2 153.6 %psum.7 = f32[2,16,128]{2,1,0:T(8,128)} all-reduce(f32[2,16,128]{2,1,0:T(8,128)S(1)} %pad_maximum_fusion.7), channel_id=1, replica_groups=mesh['lat'=32,'lon'=16] {'lat'}, use_global_device_ids=true, to_apply=%region_22.23 | all-reduce | flops 4096 | bytes 32768 | tf_op jit(solution)/shard_map/psum | solution.py:287
  (605 shorter events, 365.8 us)
Async XLA Ops:
  0.6 514.6 %copy-start = (bf16[256,512]{1,0:T(8,128)(2,1)S(1)}, bf16[256,512]{1,0:T(8,128)(2,1)}, u32[]{:S(2)}) copy-start(bf16[256,512]{1,0:T(8,128)(2,1)} %param.24) | copy-start | bytes 786436
  4.3 382.5 %collective-permute-start = (bf16[3,32,256]{2,1,0:T(8,128)(2,1)}, bf16[3,32,256]{2,1,0:T(8,128)(2,1)}, u32[]{:S(2)}, u32[]{:S(2)}) collective-permute-start(bf16[3,32,256]{2,1,0:T(8,128)(2,1)} %get-tuple-element.594), channel_id=1, source_target_pairs={{0,16},{16,32},{32,48},{48,64},{64,80},{80,96},{96,112},{112,128},... | collective-permute-start | bytes 147464 | tf_op jit(solution)/shard_map/ppermute | solution.py:20
  7.8 379.0 %collective-permute-start.1 = (bf16[3,32,256]{2,1,0:T(8,128)(2,1)}, bf16[3,32,256]{2,1,0:T(8,128)(2,1)}, u32[]{:S(2)}, u32[]{:S(2)}) collective-permute-start(bf16[3,32,256]{2,1,0:T(8,128)(2,1)} %get-tuple-element.595), channel_id=1, source_target_pairs={{16,0},{32,16},{48,32},{64,48},{80,64},{96,80},{112,96},{128,112},... | collective-permute-start | bytes 147464 | tf_op jit(solution)/shard_map/ppermute | solution.py:21
  388.2 35.9 %collective-permute-start.2 = (bf16[10,3,256]{2,1,0:T(4,128)(2,1)}, bf16[10,3,256]{2,1,0:T(4,128)(2,1)S(1)}, u32[]{:S(2)}, u32[]{:S(2)}) collective-permute-start(bf16[10,3,256]{2,1,0:T(4,128)(2,1)} %get-tuple-element.586), channel_id=1, source_target_pairs={{0,1},{1,2},{2,3},{3,4},{4,5},{5,6},{6,7},{7,8},{8,9},{9,10},{10,1... | collective-permute-start | bytes 46088 | tf_op jit(solution)/shard_map/ppermute | solution.py:20
  390.1 34.0 %collective-permute-start.3 = (bf16[10,3,256]{2,1,0:T(4,128)(2,1)}, bf16[10,3,256]{2,1,0:T(4,128)(2,1)S(1)}, u32[]{:S(2)}, u32[]{:S(2)}) collective-permute-start(bf16[10,3,256]{2,1,0:T(4,128)(2,1)} %get-tuple-element.587), channel_id=1, source_target_pairs={{1,0},{2,1},{3,2},{4,3},{5,4},{6,5},{7,6},{8,7},{9,8},{10,9},{11,1... | collective-permute-start | bytes 46088 | tf_op jit(solution)/shard_map/ppermute | solution.py:21
  440.6 18.4 %all-to-all-start = ((bf16[16,2,1024]{2,1,0:T(2,128)(2,1)}), bf16[16,2,1024]{2,1,0:T(2,128)(2,1)S(1)}, u32[]{:S(2)}, u32[]{:S(2)}) async-start(bf16[16,2,1024]{2,1,0:T(2,128)(2,1)} %reshape.958), calls=%async_computation | async-start | bytes 131072 | tf_op jit(solution)/shard_map/all_to_all | solution.py:140
  461.0 17.4 %all-to-all-start.1 = ((bf16[32,2,256]{2,1,0:T(2,128)(2,1)}), bf16[32,2,256]{2,1,0:T(2,128)(2,1)S(1)}, u32[]{:S(2)}, u32[]{:S(2)}) async-start(bf16[32,2,256]{2,1,0:T(2,128)(2,1)} %reshape.960), calls=%async_computation.1 | async-start | bytes 65536 | tf_op jit(solution)/shard_map/all_to_all | solution.py:144
  483.9 14.4 %all-to-all-start.2 = ((bf16[32,2,256]{2,1,0:T(2,128)(2,1)}), bf16[32,2,256]{2,1,0:T(2,128)(2,1)S(1)}, u32[]{:S(2)}, u32[]{:S(2)}) async-start(bf16[32,2,256]{2,1,0:T(2,128)(2,1)} %reshape.962), calls=%async_computation.2 | async-start | bytes 65536 | tf_op jit(solution)/shard_map/all_to_all | solution.py:150
  500.6 13.5 %all-to-all-start.3 = ((bf16[16,2,1024]{2,1,0:T(2,128)(2,1)}), bf16[16,2,1024]{2,1,0:T(2,128)(2,1)S(1)}, u32[]{:S(2)}, u32[]{:S(2)}) async-start(bf16[16,2,1024]{2,1,0:T(2,128)(2,1)} %reshape.964), calls=%async_computation.3 | async-start | bytes 131072 | tf_op jit(solution)/shard_map/all_to_all | solution.py:156
  519.9 13.5 %all-to-all-start.4 = ((bf16[16,2,1024]{2,1,0:T(2,128)(2,1)}), bf16[16,2,1024]{2,1,0:T(2,128)(2,1)S(1)}, u32[]{:S(2)}, u32[]{:S(2)}) async-start(bf16[16,2,1024]{2,1,0:T(2,128)(2,1)} %reshape.966), calls=%async_computation.4 | async-start | bytes 131072 | tf_op jit(solution)/shard_map/all_to_all | solution.py:140
  535.4 14.0 %all-to-all-start.5 = ((bf16[32,2,256]{2,1,0:T(2,128)(2,1)}), bf16[32,2,256]{2,1,0:T(2,128)(2,1)S(1)}, u32[]{:S(2)}, u32[]{:S(2)}) async-start(bf16[32,2,256]{2,1,0:T(2,128)(2,1)} %reshape.968), calls=%async_computation.5 | async-start | bytes 65536 | tf_op jit(solution)/shard_map/all_to_all | solution.py:144
  541.0 221.8 %copy-start.36 = (pred[10]{0:T(512)(128)(4,1)S(1)}, pred[10]{0:T(512)(128)(4,1)}, u32[]{:S(2)}) copy-start(pred[10]{0:T(512)(128)(4,1)} %copy-done.35) | copy-start | bytes 34
  549.6 213.3 %copy-start.12 = (bf16[256,256,1]{1,0,2:T(8,128)(2,1)S(1)}, bf16[256,256,1]{1,0,2:T(8,128)(2,1)}, u32[]{:S(2)}) copy-start(bf16[256,256,1]{1,0,2:T(8,128)(2,1)} %reshape.887) | copy-start | bytes 393220
  549.7 213.5 %copy-start.4 = (bf16[256,256,1]{1,0,2:T(8,128)(2,1)S(1)}, bf16[256,256,1]{1,0,2:T(8,128)(2,1)}, u32[]{:S(2)}) copy-start(bf16[256,256,1]{1,0,2:T(8,128)(2,1)} %reshape.890) | copy-start | bytes 393220
  549.9 213.5 %copy-start.5 = (bf16[256,256,1]{1,0,2:T(8,128)(2,1)S(1)}, bf16[256,256,1]{1,0,2:T(8,128)(2,1)}, u32[]{:S(2)}) copy-start(bf16[256,256,1]{1,0,2:T(8,128)(2,1)} %reshape.893) | copy-start | bytes 393220
  552.8 212.2 %copy-start.11 = (bf16[256,256,1]{1,0,2:T(8,128)(2,1)S(1)}, bf16[256,256,1]{1,0,2:T(8,128)(2,1)}, u32[]{:S(2)}) copy-start(bf16[256,256,1]{1,0,2:T(8,128)(2,1)} %copy-done.10) | copy-start | bytes 393220
  553.8 14.0 %all-to-all-start.6 = ((bf16[32,2,256]{2,1,0:T(2,128)(2,1)}), bf16[32,2,256]{2,1,0:T(2,128)(2,1)S(1)}, u32[]{:S(2)}, u32[]{:S(2)}) async-start(bf16[32,2,256]{2,1,0:T(2,128)(2,1)} %reshape.970), calls=%async_computation.6 | async-start | bytes 65536 | tf_op jit(solution)/shard_map/all_to_all | solution.py:150
  570.1 13.5 %all-to-all-start.7 = ((bf16[16,2,1024]{2,1,0:T(2,128)(2,1)}), bf16[16,2,1024]{2,1,0:T(2,128)(2,1)S(1)}, u32[]{:S(2)}, u32[]{:S(2)}) async-start(bf16[16,2,1024]{2,1,0:T(2,128)(2,1)} %reshape.972), calls=%async_computation.7 | async-start | bytes 131072 | tf_op jit(solution)/shard_map/all_to_all | solution.py:156
  577.3 188.9 %copy-start.16 = (bf16[4,7,38,32]{3,1,2,0:T(8,128)(2,1)S(1)}, bf16[4,7,38,32]{3,1,2,0:T(8,128)(2,1)}, u32[]{:S(2)}) copy-start(bf16[4,7,38,32]{3,1,2,0:T(8,128)(2,1)} %convolution_convert_fusion.7) | copy-start | bytes 204292
  584.4 182.2 %copy-start.15 = (bf16[4,7,38,32]{3,1,2,0:T(8,128)(2,1)S(1)}, bf16[4,7,38,32]{3,1,2,0:T(8,128)(2,1)}, u32[]{:S(2)}) copy-start(bf16[4,7,38,32]{3,1,2,0:T(8,128)(2,1)} %convolution_convert_fusion.6) | copy-start | bytes 204292
  586.3 10.9 %collective-permute-start.4 = (bf16[3,32,256]{2,1,0:T(8,128)(2,1)S(1)}, bf16[3,32,256]{2,1,0:T(8,128)(2,1)S(1)}, u32[]{:S(2)}, u32[]{:S(2)}) collective-permute-start(bf16[3,32,256]{2,1,0:T(8,128)(2,1)S(1)} %copy.231), channel_id=1, source_target_pairs={{0,16},{16,32},{32,48},{48,64},{64,80},{80,96},{96,112},{112,128},... | collective-permute-start | bytes 147464 | tf_op jit(solution)/shard_map/ppermute | solution.py:20
  589.9 8.9 %collective-permute-start.5 = (bf16[3,32,256]{2,1,0:T(8,128)(2,1)S(1)}, bf16[3,32,256]{2,1,0:T(8,128)(2,1)S(1)}, u32[]{:S(2)}, u32[]{:S(2)}) collective-permute-start(bf16[3,32,256]{2,1,0:T(8,128)(2,1)S(1)} %copy.232), channel_id=1, source_target_pairs={{16,0},{32,16},{48,32},{64,48},{80,64},{96,80},{112,96},{128,112},... | collective-permute-start | bytes 147464 | tf_op jit(solution)/shard_map/ppermute | solution.py:21
  598.8 164.0 %collective-permute-start.6 = (bf16[10,3,256]{2,1,0:T(4,128)(2,1)S(1)}, bf16[10,3,256]{2,1,0:T(4,128)(2,1)S(1)}, u32[]{:S(2)}, u32[]{:S(2)}) collective-permute-start(bf16[10,3,256]{2,1,0:T(4,128)(2,1)S(1)} %get-tuple-element.584), channel_id=1, source_target_pairs={{0,1},{1,2},{2,3},{3,4},{4,5},{5,6},{6,7},{7,8},{8,9},{9,10},{10,1... | collective-permute-start | bytes 46088 | tf_op jit(solution)/shard_map/ppermute | solution.py:20
  600.7 162.0 %collective-permute-start.7 = (bf16[10,3,256]{2,1,0:T(4,128)(2,1)S(1)}, bf16[10,3,256]{2,1,0:T(4,128)(2,1)S(1)}, u32[]{:S(2)}, u32[]{:S(2)}) collective-permute-start(bf16[10,3,256]{2,1,0:T(4,128)(2,1)S(1)} %get-tuple-element.585), channel_id=1, source_target_pairs={{1,0},{2,1},{3,2},{4,3},{5,4},{6,5},{7,6},{8,7},{9,8},{10,9},{11,1... | collective-permute-start | bytes 46088 | tf_op jit(solution)/shard_map/ppermute | solution.py:21
  (30 other events, 924.6 us)
where the time goes:
time: 783 us; the launch traced here: 770 us
  other arithmetic  245 us (31%)
  blocking collectives  154 us (20%)
  starting transfers between devices  86.6 us (11%)
  local copies, waits for them, and re-layouts  83.4 us (11%)
  loops' own time  82.4 us (11%)
  waiting for transfers between devices  64.8 us (8%)
  matrix products  49.1 us (6%)
    psum x1, blocking collectives, local(): grad_filter = lax.psum(jnp.stack([grad_real, grad_imag]), 'lat')  154 us
    lt x16, other arithmetic, advance(): degree < orders[:, None]  101 us
    while x112, other arithmetic  85.3 us
    another operation x1, loops' own time, legendre_table(): lax.scan(advance, (zeros, zeros), jnp.arange(degree_total, dtype=jnp.int3...  82.3 us
    ppermute x4, starting transfers between devices, padded(): after = lax.ppermute(initial, axis, down)  33.5 us
    dot_general x18, matrix products, band_matrix(): jnp.einsum('lrd,njd->lrnj', kept, picker, preferred_element_type=jnp.floa...  22.1 us
    squeeze x9, local copies, waits for them, and re-layouts, local(): dense_mix[basis_index]  20.8 us
    sqrt x32, other arithmetic, advance(): jnp.sqrt(jnp.maximum(4.0 * degree_float * degree_float - 1.0, 1.0) / jnp....  19.7 us
  transfers between devices with their start and end apart: 16, of which 9 were waited for; matrix products, arithmetic and copies ran while one was open for 42% of the time, Pallas kernels for 0%

commit v1 on v0

v1 whole, which is shorter than its diff:
```python
import math

import jax
import jax.numpy as jnp
import numpy as np
from jax import lax
from jax.experimental import pallas as pl
from jax.experimental.pallas import tpu as pltpu
from jax.sharding import PartitionSpec as P

EPSILON = 1e-05
MESH = pl.DeviceIdType.MESH
F32 = jnp.float32
BF16 = jnp.bfloat16

NLAT = 128
NLON = 512
CHANS = 256
HIDDEN = 512
BASIS = 9
GROUP = 16
TAPS = 7
REACH = 3
LATS = 32
ROWS = 4
COLS = 32
ORDERS = 4
PARTS = 8
NEAR = 8
FAR = 64


def legendre_values():
    theta = math.pi * (np.arange(NLAT) + 0.5) / NLAT
    cosine, sine = (np.cos(theta), np.sin(theta))
    table = np.zeros((NLAT, NLAT, NLAT))
    for order in range(NLAT):
        steps = np.arange(1, order + 1)
        growth = np.sum(0.5 * np.log((2.0 * steps + 1.0) / (2.0 * steps)))
        earlier = np.zeros(NLAT)
        latest = np.exp(-0.5 * math.log(4.0 * math.pi) + growth + order * np.log(sine))
        table[order, order] = latest
        for degree in range(order + 1, NLAT):
            upper = math.sqrt((4.0 * degree**2 - 1.0) / (degree**2 - order**2))
            below = degree - 1.0
            lower = math.sqrt((below**2 - order**2) / (4.0 * below**2 - 1.0))
            earlier, latest = (latest, upper * (cosine * latest - lower * earlier))
            table[order, degree] = latest
    return table.astype(np.float32).reshape(LATS, ORDERS, NLAT, NLAT)


def trig_values():
    table = np.zeros((2, ORDERS, 2, LATS, NEAR, COLS))
    order = 4 * np.arange(LATS)[None, :] + np.arange(ORDERS)[:, None]
    for half in range(2):
        for near in range(NEAR):
            lon = 32 * ((near // 2) * 4 + half * 2 + near % 2) + np.arange(COLS)
            angle = (order[:, :, None] * lon[None, None, :] % NLON) * (2.0 * math.pi / NLON)
            table[half, :, 0, :, near] = np.cos(angle)
            table[half, :, 1, :, near] = -np.sin(angle)
    return table.astype(np.float32).reshape(2, PARTS * LATS, NEAR * COLS)


def phase_values():
    order = 4 * np.arange(LATS)[:, None] + np.arange(ORDERS)[None, :]
    shift = np.arange(TAPS) - REACH
    angle = order[:, None, :] * shift[None, :, None] * (2.0 * math.pi / NLON)
    pairs = np.stack([np.cos(angle), np.sin(angle)], axis=-1).reshape(LATS, TAPS, PARTS, 1)
    return np.broadcast_to(pairs, (LATS, TAPS, PARTS, 128)).astype(np.float32).copy()


def quad_values():
    theta = math.pi * (np.arange(NLAT) + 0.5) / NLAT
    weights = (2.0 * math.pi / NLON) * (math.pi / NLAT) * np.sin(theta)
    return np.broadcast_to(weights[None], (8, NLAT)).astype(np.float32).copy()


def mm(left, right, left_dim=1, right_dim=0):
    return lax.dot_general(
        left, right, (((left_dim,), (right_dim,)), ((), ())), preferred_element_type=F32
    )


def split(values):
    high = values.astype(BF16)
    return (high, (values - high.astype(F32)).astype(BF16))


def swap_blocks(blocks, width):
    blocks = list(blocks)
    lane = lax.broadcasted_iota(jnp.int32, blocks[0].shape, 1)
    stride = 1
    while stride < len(blocks):
        keep = (lane & (stride * width)) == 0
        for at in range(len(blocks)):
            if at & stride == 0:
                low, high = (blocks[at], blocks[at | stride])
                blocks[at] = jnp.where(keep, low, pltpu.roll(high, stride * width, 1))
                blocks[at | stride] = jnp.where(keep, pltpu.roll(low, 128 - stride * width, 1), high)
        stride *= 2
    return blocks


def layer_norm(values):
    centred = values - jnp.mean(values, axis=0, keepdims=True)
    inverse = lax.rsqrt(jnp.mean(centred * centred, axis=0, keepdims=True) + EPSILON)
    return (centred * inverse, inverse)


def norm_back(normed, inverse, upstream):
    return inverse * (
        upstream
        - jnp.mean(upstream, axis=0, keepdims=True)
        - normed * jnp.mean(upstream * normed, axis=0, keepdims=True)
    )


def near_of(group):
    return ((group // 4) * 2 + group % 2, (group // 2) % 2)


def body(
    x_ref,
    cot_ref,
    basis_ref,
    ext_ref,
    filt_ref,
    quad_ref,
    mix_hbm,
    win_hbm,
    wout_hbm,
    leg_hbm,
    trig_hbm,
    phase_hbm,
    out_ref,
    gx_ref,
    gf_ref,
    send_near,
    recv_near,
    send_far,
    recv_far,
    grad_send,
    grad_recv,
    grad_row,
    grad_all,
    mix_v,
    win_v,
    wout_v,
    leg_v,
    leg_hi,
    leg_lo,
    trig_v,
    trig_hi,
    trig_lo,
    phase_v,
    taps_v,
    xt_v,
    normed_v,
    cott_v,
    dhid_v,
    wint_v,
    woutt_v,
    conv_v,
    coef_v,
    dcar_v,
    load_sem,
    send_sem,
    recv_sem,
):
    lat = lax.axis_index("lat")
    lon = lax.axis_index("lon")
    x_at, half, core = (lon // 4, lax.rem(lon // 2, 2), lax.rem(lon, 2))
    near_me = x_at * 2 + core
    far_me = half * LATS + lat
    z_me, y_me = (far_me // 8, lax.rem(far_me, 8))

    loads = []
    for index, (source, target) in enumerate(
        (
            (trig_hbm.at[half], trig_v),
            (phase_hbm.at[lat], phase_v),
            (leg_hbm.at[lat], leg_v),
            (mix_hbm.at[:, lon], mix_v),
            (win_hbm, win_v),
            (wout_hbm, wout_v),
        )
    ):
        copy = pltpu.make_async_copy(source, target, load_sem.at[index])
        copy.start()
        loads.append(copy)

    def near_peer(step):
        step = step + (step >= 4).astype(jnp.int32)
        peer = lax.rem(near_me + 4 + step, NEAR)
        return (peer, (lat, (peer // 2) * 4 + half * 2 + lax.rem(peer, 2)))

    def far_peer(step):
        step = step + (step >= 36).astype(jnp.int32)
        peer_z = lax.rem(z_me + 4 + step // 8, 8)
        peer_y = lax.rem(y_me + 4 + lax.rem(step, 8), 8)
        peer = peer_z * 8 + peer_y
        return (peer, (lax.rem(peer, LATS), x_at * 4 + (peer // LATS) * 2 + core))

    def loop(count, action):
        def run(step, carry):
            action(step)
            return carry

        lax.fori_loop(0, count, run, 0)

    barrier = pltpu.get_barrier_semaphore()

    def greet(peer_of):
        def action(step):
            peer, device = peer_of(step)
            pl.semaphore_signal(barrier, inc=1, device_id=device, device_id_type=MESH)

        return action

    loop(FAR - 1, greet(far_peer))
    loop(NEAR - 1, greet(near_peer))

    def start_near(at):
        def action(step):
            peer, device = near_peer(step)
            pltpu.make_async_remote_copy(
                src_ref=send_near.at[at, peer],
                dst_ref=recv_near.at[at, near_me],
                send_sem=send_sem.at[at],
                recv_sem=recv_sem.at[at],
                device_id=device,
                device_id_type=MESH,
            ).start()

        loop(NEAR - 1, action)
        recv_near[at, near_me] = send_near[at, near_me]

    def wait_near(at):
        block = recv_near.at[at, pl.ds(0, NEAR - 1)]
        pltpu.make_async_copy(block, block, recv_sem.at[at]).wait()

    def start_far(at, both):
        def action(step):
            peer, device = far_peer(step)
            pltpu.make_async_remote_copy(
                src_ref=send_far.at[at, lax.rem(peer, LATS) if both else peer],
                dst_ref=recv_far.at[at, far_me],
                send_sem=send_sem.at[4 + at],
                recv_sem=recv_sem.at[4 + at],
                device_id=device,
                device_id_type=MESH,
            ).start()

        loop(FAR - 1, action)
        recv_far[at, far_me] = send_far[at, lat if both else far_me]

    def wait_far(at):
        block = recv_far.at[at, pl.ds(0, FAR - 1)]
        pltpu.make_async_copy(block, block, recv_sem.at[4 + at]).wait()

    def send_field(at, field):
        for group in range(CHANS // GROUP):
            near, part = near_of(group)
            send_near[at, near, part * GROUP : (part + 1) * GROUP, :] = field[
                group * GROUP : (group + 1) * GROUP
            ].astype(BF16)
        start_near(at)

    def take_field(at):
        pieces = []
        for group in range(CHANS // GROUP):
            near, part = near_of(group)
            pieces.append(recv_near[at, near, part * GROUP : (part + 1) * GROUP, :].astype(F32))
        return jnp.concatenate(pieces, axis=0)

    def to_spectrum(near_at, far_at):
        rows = [recv_near[near_at, near].astype(F32) for near in range(NEAR)]
        first = swap_blocks(rows[:4], COLS)
        second = swap_blocks(rows[4:], COLS)
        field = jnp.concatenate(
            [jnp.concatenate([first[a], second[a]], axis=1) for a in range(ROWS)], axis=0
        ).astype(BF16)
        parts = mm(trig_hi[...], field, 1, 1) + mm(trig_lo[...], field, 1, 1)
        blocks = swap_blocks([parts[at * LATS : (at + 1) * LATS] for at in range(PARTS)], GROUP)
        flat = send_far.at[far_at].reshape(FAR * ROWS, 128)
        for a in range(ROWS):
            for part in range(2):
                flat[pl.ds(part * LATS * ROWS + a, LATS, stride=ROWS), :] = blocks[a * 2 + part]
        start_far(far_at, False)

    def take_spectrum(far_at):
        flat = recv_far.at[far_at].reshape(FAR * ROWS, 128)
        return (flat[0:NLAT, :] + flat[NLAT : 2 * NLAT, :]).T

    def send_spectrum(far_at, field):
        flat = send_far.at[far_at].reshape(FAR * ROWS, 128)
        flat[0:NLAT, :] = field.T
        start_far(far_at, True)

    def to_grid(far_at, near_at):
        flat = recv_far.at[far_at].reshape(FAR * ROWS, 128)
        rows = []
        for a in range(ROWS):
            for part in range(2):
                rows.append(flat[pl.ds(part * LATS * ROWS + a, LATS, stride=ROWS), :])
        stacked = jnp.concatenate(swap_blocks(rows, GROUP), axis=0).astype(BF16)
        field = mm(stacked, trig_hi[...], 0, 0) + mm(stacked, trig_lo[...], 0, 0)
        for side in range(2):
            blocks = swap_blocks(
                [
                    field[a * COLS : (a + 1) * COLS, side * 128 : (side + 1) * 128]
                    for a in range(ROWS)
                ],
                COLS,
            )
            for at in range(4):
                send_near[near_at, side * 4 + at] = blocks[at].astype(BF16)
        start_near(near_at)

    def analyse(rows, at):
        rows = rows.astype(BF16)
        return mm(rows, leg_hi[at], 1, 1) + mm(rows, leg_lo[at], 1, 1)

    def synthesise(rows, at):
        rows = rows.astype(BF16)
        return mm(rows, leg_hi[at]) + mm(rows, leg_lo[at])

    def order_weight(at):
        return jnp.where(lat * ORDERS + at == 0, 1.0, 2.0).astype(F32)

    xt = x_ref[...].astype(F32).T
    normed, inverse_in = layer_norm(xt)
    xt_v[...] = xt
    normed_v[...] = normed
    pl.semaphore_wait(barrier, NEAR - 1 + FAR - 1)
    send_field(0, normed)

    loads[0].wait()
    trig_hi[...], trig_lo[...] = split(trig_v[...])
    loads[1].wait()
    lat_at = lax.broadcasted_iota(jnp.int32, (TAPS, 128), 1)
    shift = lax.broadcasted_iota(jnp.int32, (TAPS, 128), 0) - REACH
    for r in range(TAPS):
        west, east = (ext_ref[r, 0:1, :], ext_ref[r, 1:2, :])
        inside = (shift >= -west) & (shift <= east)
        inside = inside & (lat_at + (r - REACH) >= 0) & (lat_at + (r - REACH) < NLAT)
        for k in range(BASIS):
            kept = jnp.where(inside, basis_ref[k, r].astype(F32), 0.0)
            total = phase_v[0] * kept[0:1]
            for d in range(1, TAPS):
                total = total + phase_v[d] * kept[d : d + 1]
            taps_v[k, r] = total
    for copy in loads[2:]:
        copy.wait()

    wait_near(0)
    to_spectrum(0, 0)

    leg_hi[...], leg_lo[...] = split(leg_v[...])
    mix = mix_v[...].reshape(BASIS * GROUP, GROUP)
    cott = cot_ref[...].astype(F32).T
    cott_v[...] = cott
    dhid_v[...] = mm(wout_v[...], cott.astype(BF16))
    wint_v[...] = win_v[...].T
    woutt_v[...] = wout_v[...].T
    quad = quad_ref[0:1, :]
    filter_real, filter_imag = (filt_ref[0], filt_ref[1])

    wait_far(0)
    spectrum = take_spectrum(0)
    for at in range(ORDERS):
        real = spectrum[at * 32 : at * 32 + 16]
        imag = spectrum[at * 32 + 16 : at * 32 + 32]
        sum_real = jnp.zeros((BASIS, GROUP, 128), F32)
        sum_imag = jnp.zeros((BASIS, GROUP, 128), F32)
        for r in range(TAPS):
            moved_real = pltpu.roll(real, (REACH - r) % 128, 1)[None]
            moved_imag = pltpu.roll(imag, (REACH - r) % 128, 1)[None]
            tap_real = taps_v[:, r, 2 * at : 2 * at + 1, :]
            tap_imag = taps_v[:, r, 2 * at + 1 : 2 * at + 2, :]
            sum_real = sum_real + (tap_real * moved_real - tap_imag * moved_imag)
            sum_imag = sum_imag + (tap_real * moved_imag + tap_imag * moved_real)
        conv_v[:, 2 * at * 128 : (2 * at + 1) * 128] = sum_real.reshape(144, 128).astype(BF16)
        conv_v[:, (2 * at + 1) * 128 : (2 * at + 2) * 128] = sum_imag.reshape(144, 128).astype(BF16)
    mixed = mm(mix, conv_v[...], 0, 0)
    pieces = []
    for at in range(ORDERS):
        rows = jnp.concatenate(
            [
                mixed[:, 2 * at * 128 : (2 * at + 1) * 128] * quad,
                mixed[:, (2 * at + 1) * 128 : (2 * at + 2) * 128] * quad,
            ],
            axis=0,
        )
        coefs = analyse(rows, at)
        coef_v[at] = coefs
        real, imag = (coefs[0:16], coefs[16:32])
        product = jnp.concatenate(
            [
                real * filter_real - imag * filter_imag,
                real * filter_imag + imag * filter_real,
            ],
            axis=0,
        )
        pieces.append(synthesise(product, at) * order_weight(at))
    send_spectrum(1, jnp.concatenate(pieces, axis=0))
    wait_far(1)
    to_grid(1, 1)
    wait_near(1)

    carried = xt_v[...] + take_field(1)
    normed_mid, inverse_mid = layer_norm(carried)
    preact = mm(wint_v[...], normed_mid.astype(BF16))
    bell = jnp.exp(-0.5 * preact * preact) * (1.0 / math.sqrt(2.0 * math.pi))
    gate = 0.5 * (1.0 + lax.erf(preact * (1.0 / math.sqrt(2.0))))
    d_preact = (dhid_v[...] * (gate + preact * bell)).astype(BF16)
    d_normed = mm(win_v[...], d_preact)
    d_carried = cott_v[...] + norm_back(normed_mid, inverse_mid, d_normed)
    send_field(2, d_carried)
    dcar_v[...] = d_carried
    hidden = (preact * gate).astype(BF16)
    output = carried + mm(woutt_v[...], hidden)
    out_ref[...] = output.T.astype(BF16)

    wait_near(2)
    to_spectrum(2, 2)
    wait_far(2)
    spectrum = take_spectrum(2)
    grad_real = jnp.zeros((GROUP, 128), F32)
    grad_imag = jnp.zeros((GROUP, 128), F32)
    pieces = []
    for at in range(ORDERS):
        upstream = analyse(spectrum[at * 32 : at * 32 + 32], at) * order_weight(at)
        up_real, up_imag = (upstream[0:16], upstream[16:32])
        real, imag = (coef_v[at, 0:16], coef_v[at, 16:32])
        grad_real = grad_real + (up_real * real + up_imag * imag)
        grad_imag = grad_imag + (up_imag * real - up_real * imag)
        d_coeff = jnp.concatenate(
            [
                up_real * filter_real + up_imag * filter_imag,
                up_imag * filter_real - up_real * filter_imag,
            ],
            axis=0,
        )
        rows = synthesise(d_coeff, at) * quad
        pieces.extend([rows[0:16], rows[16:32]])
    d_conv = mm(mix, jnp.concatenate(pieces, axis=1).astype(BF16))
    pieces = []
    for at in range(ORDERS):
        real = d_conv[:, 2 * at * 128 : (2 * at + 1) * 128].reshape(BASIS, GROUP, 128)
        imag = d_conv[:, (2 * at + 1) * 128 : (2 * at + 2) * 128].reshape(BASIS, GROUP, 128)
        sum_real = jnp.zeros((GROUP, 128), F32)
        sum_imag = jnp.zeros((GROUP, 128), F32)
        for r in range(TAPS):
            tap_real = taps_v[:, r, 2 * at : 2 * at + 1, :]
            tap_imag = taps_v[:, r, 2 * at + 1 : 2 * at + 2, :]
            row_real = jnp.sum(tap_real * real + tap_imag * imag, axis=0)
            row_imag = jnp.sum(tap_real * imag - tap_imag * real, axis=0)
            sum_real = sum_real + pltpu.roll(row_real, (r - REACH) % 128, 1)
            sum_imag = sum_imag + pltpu.roll(row_imag, (r - REACH) % 128, 1)
        pieces.extend([sum_real, sum_imag])
    send_spectrum(3, jnp.concatenate(pieces, axis=0))

    flat = grad_send.reshape(2 * GROUP, 128)
    flat[0:GROUP, :] = grad_real
    flat[GROUP : 2 * GROUP, :] = grad_imag

    def column_peer(step):
        peer = lax.rem(lat + 1 + step, LATS)
        return (peer, (peer, lon))

    def scatter(step):
        peer, device = column_peer(step)
        pltpu.make_async_remote_copy(
            src_ref=grad_send.at[peer],
            dst_ref=grad_recv.at[lat],
            send_sem=send_sem.at[8],
            recv_sem=recv_sem.at[8],
            device_id=device,
            device_id_type=MESH,
        ).start()

    def gather(step):
        peer, device = column_peer(step)
        pltpu.make_async_remote_copy(
            src_ref=grad_row.at[0],
            dst_ref=grad_all.at[lat],
            send_sem=send_sem.at[9],
            recv_sem=recv_sem.at[9],
            device_id=device,
            device_id_type=MESH,
        ).start()

    loop(LATS - 1, scatter)
    grad_recv[lat] = grad_send[lat]

    wait_far(3)
    to_grid(3, 3)

    block = grad_recv.at[pl.ds(0, LATS - 1)]
    pltpu.make_async_copy(block, block, recv_sem.at[8]).wait()
    grad_row[0] = jnp.sum(grad_recv[...], axis=0)
    loop(LATS - 1, gather)
    grad_all[lat] = grad_row[0]

    wait_near(3)
    d_normed_in = take_field(3)
    grad_x = dcar_v[...] + norm_back(normed_v[...], inverse_in, d_normed_in)
    gx_ref[...] = grad_x.T.astype(BF16)

    block = grad_all.at[pl.ds(0, LATS - 1)]
    pltpu.make_async_copy(block, block, recv_sem.at[9]).wait()
    gf_ref[...] = grad_all.reshape(2 * GROUP, 128)[...]

    for at in range(4):
        block = send_near.at[at, pl.ds(0, NEAR - 1)]
        pltpu.make_async_copy(block, block, send_sem.at[at]).wait()
        block = send_far.at[at, pl.ds(0, FAR - 1)]
        pltpu.make_async_copy(block, block, send_sem.at[4 + at]).wait()
    block = grad_send.at[pl.ds(0, LATS - 1)]
    pltpu.make_async_copy(block, block, send_sem.at[8]).wait()
    pltpu.make_async_copy(block, block, send_sem.at[9]).wait()


def local(activations, basis_weights, extents, mix_weight, spec_filter, w_in, w_out, cotangent):
    cells = ROWS * COLS
    vmem = pl.BlockSpec(memory_space=pltpu.VMEM)
    anywhere = pl.BlockSpec(memory_space=pl.ANY)
    out, grad_x, grad_filter = pl.pallas_call(
        body,
        out_shape=(
            jax.ShapeDtypeStruct((cells, CHANS), BF16),
            jax.ShapeDtypeStruct((cells, CHANS), BF16),
            jax.ShapeDtypeStruct((2 * GROUP, 128), F32),
        ),
        in_specs=[vmem] * 6 + [anywhere] * 6,
        out_specs=(vmem, vmem, vmem),
        scratch_shapes=[
            pltpu.VMEM((4, NEAR, 2 * GROUP, 128), BF16),
            pltpu.VMEM((4, NEAR, 2 * GROUP, 128), BF16),
            pltpu.VMEM((4, FAR, ROWS, 128), F32),
            pltpu.VMEM((4, FAR, ROWS, 128), F32),
            pltpu.VMEM((LATS, 1, 128), F32),
            pltpu.VMEM((LATS, 1, 128), F32),
            pltpu.VMEM((1, 1, 128), F32),
            pltpu.VMEM((LATS, 1, 128), F32),
            pltpu.VMEM((BASIS, GROUP, GROUP), BF16),
            pltpu.VMEM((CHANS, HIDDEN), BF16),
            pltpu.VMEM((HIDDEN, CHANS), BF16),
            pltpu.VMEM((ORDERS, NLAT, NLAT), F32),
            pltpu.VMEM((ORDERS, NLAT, NLAT), BF16),
            pltpu.VMEM((ORDERS, NLAT, NLAT), BF16),
            pltpu.VMEM((PARTS * LATS, NEAR * COLS), F32),
            pltpu.VMEM((PARTS * LATS, NEAR * COLS), BF16),
            pltpu.VMEM((PARTS * LATS, NEAR * COLS), BF16),
            pltpu.VMEM((TAPS, PARTS, 128), F32),
            pltpu.VMEM((BASIS, TAPS, PARTS, 128), F32),
            pltpu.VMEM((CHANS, cells), F32),
            pltpu.VMEM((CHANS, cells), F32),
            pltpu.VMEM((CHANS, cells), F32),
            pltpu.VMEM((HIDDEN, cells), F32),
            pltpu.VMEM((HIDDEN, CHANS), BF16),
            pltpu.VMEM((CHANS, HIDDEN), BF16),
            pltpu.VMEM((BASIS * GROUP, 2 * ORDERS * 128), BF16),
            pltpu.VMEM((ORDERS, 2 * GROUP, 128), F32),
            pltpu.VMEM((CHANS, cells), F32),
            pltpu.SemaphoreType.DMA((6,)),
            pltpu.SemaphoreType.DMA((10,)),
            pltpu.SemaphoreType.DMA((10,)),
        ],
        compiler_params=pltpu.CompilerParams(
            collective_id=0, has_side_effects=True, vmem_limit_bytes=48 * 1024 * 1024
        ),
        name="block",
    )(
        activations.reshape(cells, CHANS),
        cotangent.reshape(cells, CHANS),
        jnp.transpose(basis_weights, (0, 2, 3, 1)),
        jnp.transpose(extents, (2, 0, 1)),
        spec_filter,
        quad_values(),
        mix_weight,
        w_in,
        w_out,
        legendre_values(),
        trig_values(),
        phase_values(),
    )
    return (
        out.reshape(ROWS, COLS, CHANS),
        grad_x.reshape(ROWS, COLS, CHANS),
        grad_filter.reshape(2, GROUP, 128),
    )


def solution(mesh):
    placed = (
        P("lat", "lon", None),
        P(),
        P(),
        P(),
        P(None, "lon", None),
        P(),
        P(),
        P("lat", "lon", None),
    )
    return jax.shard_map(
        local,
        mesh=mesh,
        in_specs=placed,
        out_specs=(P("lat", "lon", None), P("lat", "lon", None), P(None, "lon", None)),
        check_vma=False,
    )
```

time: 783 us -> 85.9 us (0.11)
  the two profiles are of different devices: /device:TPU:2 before, /device:TPU:1 now
where the time goes in v1:
time: 85.9 us; the launch traced here: 85.3 us
  Pallas kernels  72.9 us (85%)
  local copies, waits for them, and re-layouts  11.7 us (14%)
    pallas_call x1, Pallas kernels, local(): pl.pallas_call(body, out_shape=(jax.ShapeDtypeStruct((cells, CHANS), BF16...  72.9 us
    unnamed x25, local copies, waits for them, and re-layouts  11.7 us

profile of v1, /device:TPU:1, one launch (start us, length us, event | category | flops | bytes accessed | tf_op | source)
XLA Modules:
  0.0 85.3 jit_solution(13339928982536710288)
XLA Ops:
  0.6 0.0 copy-start
  0.6 1.2 %copy-done = f32[32,7,8,128]{3,2,1,0:T(8,128)S(1)} copy-done((f32[32,7,8,128]{3,2,1,0:T(8,128)S(1)}, f32[32,7,8,128]{3,2,1,0:T(8,128)}, u32[]{:S(2)}) %copy-start) | copy-done | bytes 917528
  1.8 0.0 copy-start.1
  1.8 1.1 %copy-done.1 = bf16[9,16,16,16]{3,2,1,0:T(8,128)(2,1)S(1)} copy-done((bf16[9,16,16,16]{3,2,1,0:T(8,128)(2,1)S(1)}, bf16[9,16,16,16]{3,2,1,0:T(8,128)(2,1)}, u32[]{:S(2)}) %copy-start.1) | copy-done | bytes 73752
  2.9 0.0 copy-start.2
  2.9 1.0 %copy-done.2 = f32[2,256,256]{2,1,0:T(8,128)S(1)} copy-done((f32[2,256,256]{2,1,0:T(8,128)S(1)}, f32[2,256,256]{2,1,0:T(8,128)}, u32[]{:S(2)}) %copy-start.2) | copy-done | bytes 524312
  3.9 0.0 copy-start.3
  3.9 0.9 %copy-done.3 = bf16[256,512]{1,0:T(8,128)(2,1)S(1)} copy-done((bf16[256,512]{1,0:T(8,128)(2,1)S(1)}, bf16[256,512]{1,0:T(8,128)(2,1)}, u32[]{:S(2)}) %copy-start.3) | copy-done | bytes 262168
  4.9 0.0 copy-start.4
  4.9 0.9 %copy-done.4 = bf16[512,256]{1,0:T(8,128)(2,1)S(1)} copy-done((bf16[512,256]{1,0:T(8,128)(2,1)S(1)}, bf16[512,256]{1,0:T(8,128)(2,1)}, u32[]{:S(2)}) %copy-start.4) | copy-done | bytes 262168
  5.8 0.0 copy-start.5
  5.8 0.9 %copy-done.5 = bf16[9,128,7,7]{1,3,2,0:T(8,128)(2,1)S(1)} copy-done((bf16[9,128,7,7]{1,3,2,0:T(8,128)(2,1)S(1)}, bf16[9,128,7,7]{1,3,2,0:T(8,128)(2,1)}, u32[]{:S(2)}) %copy-start.5) | copy-done | bytes 112920
  6.7 0.0 copy-start.6
  6.7 0.8 copy-done.6
  7.6 0.0 copy-start.7
  7.6 0.8 copy-done.7
  8.4 0.0 copy-start.8
  8.4 0.7 copy-done.8
  9.1 0.7 copy-done.9
  9.8 0.7 copy-done.10
  10.5 72.9 %block.1 = (bf16[128,256]{1,0:T(8,128)(2,1)S(1)}, bf16[128,256]{1,0:T(8,128)(2,1)S(1)}, f32[32,128]{1,0:T(8,128)S(1)}) custom-call(bf16[128,256]{1,0:T(8,128)(2,1)S(1)} %bitcast.8, bf16[128,256]{1,0:T(8,128)(2,1)S(1)} %bitcast.9, bf16[9,7,7,128]{3,2,1,0:T(8,128)(2,1)S(1)} %bitcast.7, s32[7,2,128]{2,1,0:T(2,128)S(1)} %bitcast.13, ...), custom_call_target="tpu_custom_call" | custom-call | tf_op jit(solution)/shard_map/block/pallas_call | solution.py:529
  83.4 0.6 copy.18
  84.1 0.6 copy.19
  84.7 0.6 copy.20
  (2 shorter events, 0.0 us)
Async XLA Ops:
  0.6 1.2 %copy-start = (f32[32,7,8,128]{3,2,1,0:T(8,128)S(1)}, f32[32,7,8,128]{3,2,1,0:T(8,128)}, u32[]{:S(2)}) copy-start(f32[32,7,8,128]{3,2,1,0:T(8,128)} %constant.11.clone.phase_hbm) | copy-start | bytes 2752516
  1.8 1.1 %copy-start.1 = (bf16[9,16,16,16]{3,2,1,0:T(8,128)(2,1)S(1)}, bf16[9,16,16,16]{3,2,1,0:T(8,128)(2,1)}, u32[]{:S(2)}) copy-start(bf16[9,16,16,16]{3,2,1,0:T(8,128)(2,1)} %mix_hbm.1) | copy-start | bytes 221188
  2.9 1.0 %copy-start.2 = (f32[2,256,256]{2,1,0:T(8,128)S(1)}, f32[2,256,256]{2,1,0:T(8,128)}, u32[]{:S(2)}) copy-start(f32[2,256,256]{2,1,0:T(8,128)} %constant.10.clone.trig_hbm) | copy-start | bytes 1572868
  3.9 0.9 %copy-start.3 = (bf16[256,512]{1,0:T(8,128)(2,1)S(1)}, bf16[256,512]{1,0:T(8,128)(2,1)}, u32[]{:S(2)}) copy-start(bf16[256,512]{1,0:T(8,128)(2,1)} %win_hbm.1) | copy-start | bytes 786436
  4.9 0.9 %copy-start.4 = (bf16[512,256]{1,0:T(8,128)(2,1)S(1)}, bf16[512,256]{1,0:T(8,128)(2,1)}, u32[]{:S(2)}) copy-start(bf16[512,256]{1,0:T(8,128)(2,1)} %wout_hbm.1) | copy-start | bytes 786436
  5.8 0.9 %copy-start.5 = (bf16[9,128,7,7]{1,3,2,0:T(8,128)(2,1)S(1)}, bf16[9,128,7,7]{1,3,2,0:T(8,128)(2,1)}, u32[]{:S(2)}) copy-start(bf16[9,128,7,7]{1,3,2,0:T(8,128)(2,1)} %param.13) | copy-start | bytes 338692
  6.7 0.8 copy-start.6
  7.6 0.8 copy-start.7
  8.4 0.7 copy-start.8
  9.1 0.7 copy-start.9
  9.8 0.7 copy-start.10

commit v2 on v1

--- a/solution.py
+++ b/solution.py
@@ -28,6 +28,7 @@
 PARTS = 8
 NEAR = 8
 FAR = 64
+FARTHEST = (4, 3, 5, 2, 6, 1, 7, 0)
 
 
 def legendre_values():
@@ -120,18 +121,18 @@
 
 
 def body(
-    x_ref,
-    cot_ref,
-    basis_ref,
-    ext_ref,
-    filt_ref,
-    quad_ref,
+    x_hbm,
+    cot_hbm,
+    basis_hbm,
+    ext_hbm,
+    filt_hbm,
     mix_hbm,
     win_hbm,
     wout_hbm,
     leg_hbm,
     trig_hbm,
     phase_hbm,
+    quad_hbm,
     out_ref,
     gx_ref,
     gf_ref,
@@ -163,7 +164,14 @@
     conv_v,
     coef_v,
     dcar_v,
+    x_ref,
+    cot_ref,
+    basis_ref,
+    ext_ref,
+    filt_ref,
+    quad_ref,
     load_sem,
+    ring_sem,
     send_sem,
     recv_sem,
 ):
@@ -177,12 +185,18 @@
     loads = []
     for index, (source, target) in enumerate(
         (
+            (x_hbm, x_ref),
+            (ext_hbm, ext_ref),
+            (basis_hbm, basis_ref),
             (trig_hbm.at[half], trig_v),
             (phase_hbm.at[lat], phase_v),
             (leg_hbm.at[lat], leg_v),
             (mix_hbm.at[:, lon], mix_v),
             (win_hbm, win_v),
             (wout_hbm, wout_v),
+            (cot_hbm, cot_ref),
+            (filt_hbm, filt_ref),
+            (quad_hbm, quad_ref),
         )
     ):
         copy = pltpu.make_async_copy(source, target, load_sem.at[index])
@@ -194,13 +208,6 @@
         peer = lax.rem(near_me + 4 + step, NEAR)
         return (peer, (lat, (peer // 2) * 4 + half * 2 + lax.rem(peer, 2)))
 
-    def far_peer(step):
-        step = step + (step >= 36).astype(jnp.int32)
-        peer_z = lax.rem(z_me + 4 + step // 8, 8)
-        peer_y = lax.rem(y_me + 4 + lax.rem(step, 8), 8)
-        peer = peer_z * 8 + peer_y
-        return (peer, (lax.rem(peer, LATS), x_at * 4 + (peer // LATS) * 2 + core))
-
     def loop(count, action):
         def run(step, carry):
             action(step)
@@ -208,17 +215,37 @@
 
         lax.fori_loop(0, count, run, 0)
 
+    far_y = [lax.rem(y_me + move, 8) for move in FARTHEST]
+
+    def far_device(peer_z, peer_y):
+        peer_lat = lax.rem(peer_z, 4) * 8 + peer_y
+        peer_lon = x_at * 4 + (peer_z // 4) * 2 + core
+        return (peer_z * 8 + peer_y, peer_lat, (peer_lat, peer_lon))
+
+    def over_far(action):
+        def plane(step):
+            away = (step + 1) // 2
+            peer_z = lax.rem(z_me + 4 + away * (1 - 2 * lax.rem(step, 2)), 8)
+            for peer_y in far_y:
+                action(*far_device(peer_z, peer_y))
+
+        loop(7, plane)
+        for peer_y in far_y[:-1]:
+            action(*far_device(z_me, peer_y))
+
+    def ring_z(move):
+        return far_device(lax.rem(z_me + move, 8), y_me)[2]
+
     barrier = pltpu.get_barrier_semaphore()
 
-    def greet(peer_of):
-        def action(step):
-            peer, device = peer_of(step)
-            pl.semaphore_signal(barrier, inc=1, device_id=device, device_id_type=MESH)
-
-        return action
-
-    loop(FAR - 1, greet(far_peer))
-    loop(NEAR - 1, greet(near_peer))
+    def greet(device):
+        pl.semaphore_signal(barrier, inc=1, device_id=device, device_id_type=MESH)
+
+    for move in FARTHEST[:-1]:
+        greet(ring_z(move))
+    for peer_y in far_y[:-1]:
+        greet(far_device(z_me, peer_y)[2])
+    loop(NEAR - 1, lambda step: greet(near_peer(step)[1]))
 
     def start_near(at):
         def action(step):
@@ -240,10 +267,9 @@
         pltpu.make_async_copy(block, block, recv_sem.at[at]).wait()
 
     def start_far(at, both):
-        def action(step):
-            peer, device = far_peer(step)
+        def action(peer, peer_lat, device):
             pltpu.make_async_remote_copy(
-                src_ref=send_far.at[at, lax.rem(peer, LATS) if both else peer],
+                src_ref=send_far.at[at, peer_lat if both else peer],
                 dst_ref=recv_far.at[at, far_me],
                 send_sem=send_sem.at[4 + at],
                 recv_sem=recv_sem.at[4 + at],
@@ -251,7 +277,7 @@
                 device_id_type=MESH,
             ).start()
 
-        loop(FAR - 1, action)
+        over_far(action)
         recv_far[at, far_me] = send_far[at, lat if both else far_me]
 
     def wait_far(at):
@@ -286,6 +312,8 @@
         for a in range(ROWS):
             for part in range(2):
                 flat[pl.ds(part * LATS * ROWS + a, LATS, stride=ROWS), :] = blocks[a * 2 + part]
+        if far_at == 0:
+            pl.semaphore_wait(ring_sem, 7)
         start_far(far_at, False)
 
     def take_spectrum(far_at):
@@ -328,16 +356,19 @@
     def order_weight(at):
         return jnp.where(lat * ORDERS + at == 0, 1.0, 2.0).astype(F32)
 
+    loads[0].wait()
     xt = x_ref[...].astype(F32).T
     normed, inverse_in = layer_norm(xt)
     xt_v[...] = xt
     normed_v[...] = normed
-    pl.semaphore_wait(barrier, NEAR - 1 + FAR - 1)
+    pl.semaphore_wait(barrier, NEAR - 1 + 7 + 7)
+    for move in FARTHEST[:-1]:
+        pl.semaphore_signal(ring_sem, inc=1, device_id=ring_z(move), device_id_type=MESH)
     send_field(0, normed)
 
-    loads[0].wait()
+    for copy in loads[1:5]:
+        copy.wait()
     trig_hi[...], trig_lo[...] = split(trig_v[...])
-    loads[1].wait()
     lat_at = lax.broadcasted_iota(jnp.int32, (TAPS, 128), 1)
     shift = lax.broadcasted_iota(jnp.int32, (TAPS, 128), 0) - REACH
     for r in range(TAPS):
@@ -350,7 +381,7 @@
             for d in range(1, TAPS):
                 total = total + phase_v[d] * kept[d : d + 1]
             taps_v[k, r] = total
-    for copy in loads[2:]:
+    for copy in loads[5:]:
         copy.wait()
 
     wait_near(0)
@@ -525,7 +556,7 @@
 def local(activations, basis_weights, extents, mix_weight, spec_filter, w_in, w_out, cotangent):
     cells = ROWS * COLS
     vmem = pl.BlockSpec(memory_space=pltpu.VMEM)
-    anywhere = pl.BlockSpec(memory_space=pl.ANY)
+    hbm = pl.BlockSpec(memory_space=pltpu.HBM)
     out, grad_x, grad_filter = pl.pallas_call(
         body,
         out_shape=(
@@ -533,7 +564,7 @@
             jax.ShapeDtypeStruct((cells, CHANS), BF16),
             jax.ShapeDtypeStruct((2 * GROUP, 128), F32),
         ),
-        in_specs=[vmem] * 6 + [anywhere] * 6,
+        in_specs=[hbm] * 12,
         out_specs=(vmem, vmem, vmem),
         scratch_shapes=[
             pltpu.VMEM((4, NEAR, 2 * GROUP, 128), BF16),
@@ -564,12 +595,19 @@
             pltpu.VMEM((BASIS * GROUP, 2 * ORDERS * 128), BF16),
             pltpu.VMEM((ORDERS, 2 * GROUP, 128), F32),
             pltpu.VMEM((CHANS, cells), F32),
-            pltpu.SemaphoreType.DMA((6,)),
+            pltpu.VMEM((cells, CHANS), BF16),
+            pltpu.VMEM((cells, CHANS), BF16),
+            pltpu.VMEM((BASIS, TAPS, TAPS, NLAT), BF16),
+            pltpu.VMEM((TAPS, 2, NLAT), jnp.int32),
+            pltpu.VMEM((2, GROUP, NLAT), F32),
+            pltpu.VMEM((8, NLAT), F32),
+            pltpu.SemaphoreType.DMA((12,)),
+            pltpu.SemaphoreType.REGULAR,
             pltpu.SemaphoreType.DMA((10,)),
             pltpu.SemaphoreType.DMA((10,)),
         ],
         compiler_params=pltpu.CompilerParams(
-            collective_id=0, has_side_effects=True, vmem_limit_bytes=48 * 1024 * 1024
+            collective_id=0, has_side_effects=True, vmem_limit_bytes=60 * 1024 * 1024
         ),
         name="block",
     )(
@@ -578,13 +616,13 @@
         jnp.transpose(basis_weights, (0, 2, 3, 1)),
         jnp.transpose(extents, (2, 0, 1)),
         spec_filter,
-        quad_values(),
         mix_weight,
         w_in,
         w_out,
         legendre_values(),
         trig_values(),
         phase_values(),
+        quad_values(),
     )
     return (
         out.reshape(ROWS, COLS, CHANS),

time: 85.9 us -> 72.2 us (0.84)
  local copies, waits for them, and re-layouts: 11.7 us -> 4.27 us
  Pallas kernels: 72.9 us -> 66.3 us
    unnamed x25 -> x3, local copies, waits for them, and re-layouts: 11.7 us -> 4.27 us
    pallas_call x1, Pallas kernels: 72.9 us -> 66.3 us  [local(): pl.pallas_call(body, out_shape=(jax.ShapeDtypeStruct((cells, CHANS), BF16...]
where the time goes in v2:
time: 72.2 us; the launch traced here: 71.2 us
  Pallas kernels  66.3 us (92%)
  local copies, waits for them, and re-layouts  4.27 us (6%)
    pallas_call x1, Pallas kernels, local(): pl.pallas_call(body, out_shape=(jax.ShapeDtypeStruct((cells, CHANS), BF16...  66.3 us
    unnamed x3, local copies, waits for them, and re-layouts  4.27 us

profile of v2, /device:TPU:1, one launch (start us, length us, event | category | flops | bytes accessed | tf_op | source)
XLA Modules:
  0.0 71.2 jit_solution(1498418463126426648)
XLA Ops:
  0.6 66.3 %block.1 = (bf16[128,256]{1,0:T(8,128)(2,1)}, bf16[128,256]{1,0:T(8,128)(2,1)}, f32[32,128]{1,0:T(8,128)}) custom-call(bf16[128,256]{1,0:T(8,128)(2,1)} %bitcast.8, bf16[128,256]{1,0:T(8,128)(2,1)} %bitcast.9, bf16[9,7,7,128]{3,2,1,0:T(8,128)(2,1)} %bitcast.7, s32[7,2,128]{2,1,0:T(2,128)} %bitcast.13, f32[2,16,128]{2,1,0:T(8,128)} %filt_hbm.1, ...), custom_call_target="tpu_custom_call" | custom-call | tf_op jit(solution)/shard_map/block/pallas_call | solution.py:560
  67.0 1.5 %copy.18 = bf16[4,32,256]{2,1,0:T(8,128)(2,1)} copy(bf16[4,32,256]{2,1,0:T(8,128)(2,1)} %bitcast.11) | data formatting | bytes 131072
  68.4 1.5 %copy.19 = bf16[4,32,256]{2,1,0:T(8,128)(2,1)} copy(bf16[4,32,256]{2,1,0:T(8,128)(2,1)} %bitcast.10) | data formatting | bytes 131072
  69.9 1.3 %copy.20 = f32[2,16,128]{2,1,0:T(8,128)} copy(f32[2,16,128]{2,1,0:T(8,128)} %bitcast.12) | data formatting | bytes 32768

commit v3 on v2

--- a/solution.py
+++ b/solution.py
@@ -133,9 +133,9 @@
     trig_hbm,
     phase_hbm,
     quad_hbm,
-    out_ref,
-    gx_ref,
-    gf_ref,
+    out_hbm,
+    gx_hbm,
+    gf_hbm,
     send_near,
     recv_near,
     send_far,
@@ -148,11 +148,11 @@
     win_v,
     wout_v,
     leg_v,
-    leg_hi,
-    leg_lo,
+    leg_in,
+    leg_out,
     trig_v,
-    trig_hi,
-    trig_lo,
+    trig_down,
+    trig_wide,
     phase_v,
     taps_v,
     xt_v,
@@ -170,7 +170,11 @@
     ext_ref,
     filt_ref,
     quad_ref,
+    out_ref,
+    gx_ref,
+    gf_ref,
     load_sem,
+    store_sem,
     ring_sem,
     send_sem,
     recv_sem,
@@ -306,7 +310,8 @@
         field = jnp.concatenate(
             [jnp.concatenate([first[a], second[a]], axis=1) for a in range(ROWS)], axis=0
         ).astype(BF16)
-        parts = mm(trig_hi[...], field, 1, 1) + mm(trig_lo[...], field, 1, 1)
+        parts = mm(trig_down[...], field, 1, 1)
+        parts = parts[0 : PARTS * LATS] + parts[PARTS * LATS :]
         blocks = swap_blocks([parts[at * LATS : (at + 1) * LATS] for at in range(PARTS)], GROUP)
         flat = send_far.at[far_at].reshape(FAR * ROWS, 128)
         for a in range(ROWS):
@@ -332,7 +337,8 @@
             for part in range(2):
                 rows.append(flat[pl.ds(part * LATS * ROWS + a, LATS, stride=ROWS), :])
         stacked = jnp.concatenate(swap_blocks(rows, GROUP), axis=0).astype(BF16)
-        field = mm(stacked, trig_hi[...], 0, 0) + mm(stacked, trig_lo[...], 0, 0)
+        field = mm(stacked, trig_wide[...], 0, 0)
+        field = field[:, 0 : NEAR * COLS] + field[:, NEAR * COLS :]
         for side in range(2):
             blocks = swap_blocks(
                 [
@@ -346,12 +352,12 @@
         start_near(near_at)
 
     def analyse(rows, at):
-        rows = rows.astype(BF16)
-        return mm(rows, leg_hi[at], 1, 1) + mm(rows, leg_lo[at], 1, 1)
+        both = mm(rows.astype(BF16), leg_in[at])
+        return both[:, 0:NLAT] + both[:, NLAT:]
 
     def synthesise(rows, at):
-        rows = rows.astype(BF16)
-        return mm(rows, leg_hi[at]) + mm(rows, leg_lo[at])
+        both = mm(rows.astype(BF16), leg_out[at])
+        return both[:, 0:NLAT] + both[:, NLAT:]
 
     def order_weight(at):
         return jnp.where(lat * ORDERS + at == 0, 1.0, 2.0).astype(F32)
@@ -362,13 +368,17 @@
     xt_v[...] = xt
     normed_v[...] = normed
     pl.semaphore_wait(barrier, NEAR - 1 + 7 + 7)
+    send_field(0, normed)
     for move in FARTHEST[:-1]:
         pl.semaphore_signal(ring_sem, inc=1, device_id=ring_z(move), device_id_type=MESH)
-    send_field(0, normed)
 
     for copy in loads[1:5]:
         copy.wait()
-    trig_hi[...], trig_lo[...] = split(trig_v[...])
+    high, low = split(trig_v[...])
+    trig_down[0 : PARTS * LATS] = high
+    trig_down[PARTS * LATS :] = low
+    trig_wide[:, 0 : NEAR * COLS] = high
+    trig_wide[:, NEAR * COLS :] = low
     lat_at = lax.broadcasted_iota(jnp.int32, (TAPS, 128), 1)
     shift = lax.broadcasted_iota(jnp.int32, (TAPS, 128), 0) - REACH
     for r in range(TAPS):
@@ -387,7 +397,13 @@
     wait_near(0)
     to_spectrum(0, 0)
 
-    leg_hi[...], leg_lo[...] = split(leg_v[...])
+    for at in range(ORDERS):
+        high, low = split(leg_v[at])
+        leg_out[at, :, 0:NLAT] = high
+        leg_out[at, :, NLAT:] = low
+        high, low = split(leg_v[at].T)
+        leg_in[at, :, 0:NLAT] = high
+        leg_in[at, :, NLAT:] = low
     mix = mix_v[...].reshape(BASIS * GROUP, GROUP)
     cott = cot_ref[...].astype(F32).T
     cott_v[...] = cott
@@ -452,6 +468,8 @@
     hidden = (preact * gate).astype(BF16)
     output = carried + mm(woutt_v[...], hidden)
     out_ref[...] = output.T.astype(BF16)
+    store_out = pltpu.make_async_copy(out_ref, out_hbm, store_sem.at[0])
+    store_out.start()
 
     wait_near(2)
     to_spectrum(2, 2)
@@ -459,13 +477,51 @@
     spectrum = take_spectrum(2)
     grad_real = jnp.zeros((GROUP, 128), F32)
     grad_imag = jnp.zeros((GROUP, 128), F32)
-    pieces = []
+    upstreams = []
     for at in range(ORDERS):
         upstream = analyse(spectrum[at * 32 : at * 32 + 32], at) * order_weight(at)
         up_real, up_imag = (upstream[0:16], upstream[16:32])
+        upstreams.append((up_real, up_imag))
         real, imag = (coef_v[at, 0:16], coef_v[at, 16:32])
         grad_real = grad_real + (up_real * real + up_imag * imag)
         grad_imag = grad_imag + (up_imag * real - up_real * imag)
+
+    flat = grad_send.reshape(2 * GROUP, 128)
+    flat[0:GROUP, :] = grad_real
+    flat[GROUP : 2 * GROUP, :] = grad_imag
+
+    def column_peer(step):
+        peer = lax.rem(lat + 1 + step, LATS)
+        return (peer, (peer, lon))
+
+    def scatter(step):
+        peer, device = column_peer(step)
+        pltpu.make_async_remote_copy(
+            src_ref=grad_send.at[peer],
+            dst_ref=grad_recv.at[lat],
+            send_sem=send_sem.at[8],
+            recv_sem=recv_sem.at[8],
+            device_id=device,
+            device_id_type=MESH,
+        ).start()
+
+    def gather(step):
+        peer, device = column_peer(step)
+        pltpu.make_async_remote_copy(
+            src_ref=grad_row.at[0],
+            dst_ref=grad_all.at[lat],
+            send_sem=send_sem.at[9],
+            recv_sem=recv_sem.at[9],
+            device_id=device,
+            device_id_type=MESH,
+        ).start()
+
+    loop(LATS - 1, scatter)
+    grad_recv[lat] = grad_send[lat]
+
+    pieces = []
+    for at in range(ORDERS):
+        up_real, up_imag = upstreams[at]
         d_coeff = jnp.concatenate(
             [
                 up_real * filter_real + up_imag * filter_imag,
@@ -492,56 +548,27 @@
         pieces.extend([sum_real, sum_imag])
     send_spectrum(3, jnp.concatenate(pieces, axis=0))
 
-    flat = grad_send.reshape(2 * GROUP, 128)
-    flat[0:GROUP, :] = grad_real
-    flat[GROUP : 2 * GROUP, :] = grad_imag
-
-    def column_peer(step):
-        peer = lax.rem(lat + 1 + step, LATS)
-        return (peer, (peer, lon))
-
-    def scatter(step):
-        peer, device = column_peer(step)
-        pltpu.make_async_remote_copy(
-            src_ref=grad_send.at[peer],
-            dst_ref=grad_recv.at[lat],
-            send_sem=send_sem.at[8],
-            recv_sem=recv_sem.at[8],
-            device_id=device,
-            device_id_type=MESH,
-        ).start()
-
-    def gather(step):
-        peer, device = column_peer(step)
-        pltpu.make_async_remote_copy(
-            src_ref=grad_row.at[0],
-            dst_ref=grad_all.at[lat],
-            send_sem=send_sem.at[9],
-            recv_sem=recv_sem.at[9],
-            device_id=device,
-            device_id_type=MESH,
-        ).start()
-
-    loop(LATS - 1, scatter)
-    grad_recv[lat] = grad_send[lat]
-
-    wait_far(3)
-    to_grid(3, 3)
-
     block = grad_recv.at[pl.ds(0, LATS - 1)]
     pltpu.make_async_copy(block, block, recv_sem.at[8]).wait()
     grad_row[0] = jnp.sum(grad_recv[...], axis=0)
     loop(LATS - 1, gather)
     grad_all[lat] = grad_row[0]
 
+    wait_far(3)
+    to_grid(3, 3)
+
     wait_near(3)
     d_normed_in = take_field(3)
     grad_x = dcar_v[...] + norm_back(normed_v[...], inverse_in, d_normed_in)
     gx_ref[...] = grad_x.T.astype(BF16)
+    store_gx = pltpu.make_async_copy(gx_ref, gx_hbm, store_sem.at[1])
+    store_gx.start()
 
     block = grad_all.at[pl.ds(0, LATS - 1)]
     pltpu.make_async_copy(block, block, recv_sem.at[9]).wait()
     gf_ref[...] = grad_all.reshape(2 * GROUP, 128)[...]
+    store_gf = pltpu.make_async_copy(gf_ref, gf_hbm, store_sem.at[2])
+    store_gf.start()
 
     for at in range(4):
         block = send_near.at[at, pl.ds(0, NEAR - 1)]
@@ -551,6 +578,15 @@
     block = grad_send.at[pl.ds(0, LATS - 1)]
     pltpu.make_async_copy(block, block, send_sem.at[8]).wait()
     pltpu.make_async_copy(block, block, send_sem.at[9]).wait()
+    store_out.wait()
+    store_gx.wait()
+    store_gf.wait()
+
+
+def hand_out(first, second, third, first_out, second_out, third_out):
+    first_out[...] = first[...]
+    second_out[...] = second[...]
+    third_out[...] = third[...]
 
 
 def local(activations, basis_weights, extents, mix_weight, spec_filter, w_in, w_out, cotangent):
@@ -565,7 +601,7 @@
             jax.ShapeDtypeStruct((2 * GROUP, 128), F32),
         ),
         in_specs=[hbm] * 12,
-        out_specs=(vmem, vmem, vmem),
+        out_specs=(hbm, hbm, hbm),
         scratch_shapes=[
             pltpu.VMEM((4, NEAR, 2 * GROUP, 128), BF16),
             pltpu.VMEM((4, NEAR, 2 * GROUP, 128), BF16),
@@ -579,11 +615,11 @@
             pltpu.VMEM((CHANS, HIDDEN), BF16),
             pltpu.VMEM((HIDDEN, CHANS), BF16),
             pltpu.VMEM((ORDERS, NLAT, NLAT), F32),
-            pltpu.VMEM((ORDERS, NLAT, NLAT), BF16),
-            pltpu.VMEM((ORDERS, NLAT, NLAT), BF16),
+            pltpu.VMEM((ORDERS, NLAT, 2 * NLAT), BF16),
+            pltpu.VMEM((ORDERS, NLAT, 2 * NLAT), BF16),
             pltpu.VMEM((PARTS * LATS, NEAR * COLS), F32),
-            pltpu.VMEM((PARTS * LATS, NEAR * COLS), BF16),
-            pltpu.VMEM((PARTS * LATS, NEAR * COLS), BF16),
+            pltpu.VMEM((2 * PARTS * LATS, NEAR * COLS), BF16),
+            pltpu.VMEM((PARTS * LATS, 2 * NEAR * COLS), BF16),
             pltpu.VMEM((TAPS, PARTS, 128), F32),
             pltpu.VMEM((BASIS, TAPS, PARTS, 128), F32),
             pltpu.VMEM((CHANS, cells), F32),
@@ -601,7 +637,11 @@
             pltpu.VMEM((TAPS, 2, NLAT), jnp.int32),
             pltpu.VMEM((2, GROUP, NLAT), F32),
             pltpu.VMEM((8, NLAT), F32),
+            pltpu.VMEM((cells, CHANS), BF16),
+            pltpu.VMEM((cells, CHANS), BF16),
+            pltpu.VMEM((2 * GROUP, 128), F32),
             pltpu.SemaphoreType.DMA((12,)),
+            pltpu.SemaphoreType.DMA((3,)),
             pltpu.SemaphoreType.REGULAR,
             pltpu.SemaphoreType.DMA((10,)),
             pltpu.SemaphoreType.DMA((10,)),
@@ -624,6 +664,17 @@
         phase_values(),
         quad_values(),
     )
+    out, grad_x, grad_filter = pl.pallas_call(
+        hand_out,
+        out_shape=(
+            jax.ShapeDtypeStruct((cells, CHANS), BF16),
+            jax.ShapeDtypeStruct((cells, CHANS), BF16),
+            jax.ShapeDtypeStruct((2 * GROUP, 128), F32),
+        ),
+        in_specs=[vmem] * 3,
+        out_specs=(vmem,) * 3,
+        name="hand_out",
+    )(out, grad_x, grad_filter)
     return (
         out.reshape(ROWS, COLS, CHANS),
         grad_x.reshape(ROWS, COLS, CHANS),

time: 72.2 us -> 67.9 us (0.940); the launches traced: 71.2 us -> 67.7 us
  local copies, waits for them, and re-layouts: 4.27 us -> 0 us
  Pallas kernels: 66.3 us -> 67.1 us
    unnamed x3 -> x0, local copies, waits for them, and re-layouts: 4.27 us -> none
    pallas_call x0 -> x1, Pallas kernels: none -> 1.53 us  [local(): pl.pallas_call(hand_out, out_shape=(jax.ShapeDtypeStruct((cells, CHANS),...]
    pallas_call x1, Pallas kernels: 66.3 us -> 65.6 us  [local(): pl.pallas_call(body, out_shape=(jax.ShapeDtypeStruct((cells, CHANS), BF16...]
where the time goes in v3:
time: 67.9 us; the launch traced here: 67.7 us
  Pallas kernels  67.1 us (99%)
    pallas_call x1, Pallas kernels, local(): pl.pallas_call(body, out_shape=(jax.ShapeDtypeStruct((cells, CHANS), BF16...  65.6 us
    pallas_call x1, Pallas kernels, local(): pl.pallas_call(hand_out, out_shape=(jax.ShapeDtypeStruct((cells, CHANS),...  1.53 us

profile of v3, /device:TPU:1, one launch (start us, length us, event | category | flops | bytes accessed | tf_op | source)
XLA Modules:
  0.0 67.7 jit_solution(14090284024390623938)
XLA Ops:
  0.6 65.6 %block.1 = (bf16[128,256]{1,0:T(8,128)(2,1)}, bf16[128,256]{1,0:T(8,128)(2,1)}, f32[32,128]{1,0:T(8,128)}) custom-call(bf16[128,256]{1,0:T(8,128)(2,1)} %bitcast.8, bf16[128,256]{1,0:T(8,128)(2,1)} %bitcast.9, bf16[9,7,7,128]{3,2,1,0:T(8,128)(2,1)} %bitcast.7, s32[7,2,128]{2,1,0:T(2,128)} %bitcast.10, f32[2,16,128]{2,1,0:T(8,128)} %filt_hbm.1, ...), custom_call_target="tpu_custom_call" | custom-call | tf_op jit(solution)/shard_map/block/pallas_call | solution.py:596
  66.2 1.5 %hand_out.1 = (bf16[128,256]{1,0:T(8,128)(2,1)}, bf16[128,256]{1,0:T(8,128)(2,1)}, f32[32,128]{1,0:T(8,128)}) custom-call(bf16[128,256]{1,0:T(8,128)(2,1)} %get-tuple-element.9.first, bf16[128,256]{1,0:T(8,128)(2,1)} %get-tuple-element.10.second, f32[32,128]{1,0:T(8,128)} %get-tuple-element.11.third), custom_call_target="tpu_custom_call" | custom-call | tf_op jit(solution)/shard_map/hand_out/pallas_call | solution.py:667

commit v4 on v3

--- a/solution.py
+++ b/solution.py
@@ -28,6 +28,9 @@
 PARTS = 8
 NEAR = 8
 FAR = 64
+FIELD_STEPS = ((1, 16), (2, 64))
+NEAREST = (4, 5, 3, 2, 6, 1, 7)
+ORDER_STEPS = ((1, 16), (2, 32), (4, 64))
 FARTHEST = (4, 3, 5, 2, 6, 1, 7, 0)
 
 
@@ -87,37 +90,31 @@
     return (high, (values - high.astype(F32)).astype(BF16))
 
 
-def swap_blocks(blocks, width):
+def swap_blocks(blocks, steps):
     blocks = list(blocks)
     lane = lax.broadcasted_iota(jnp.int32, blocks[0].shape, 1)
-    stride = 1
-    while stride < len(blocks):
-        keep = (lane & (stride * width)) == 0
+    for stride, width in steps:
+        keep = (lane & width) == 0
         for at in range(len(blocks)):
             if at & stride == 0:
                 low, high = (blocks[at], blocks[at | stride])
-                blocks[at] = jnp.where(keep, low, pltpu.roll(high, stride * width, 1))
-                blocks[at | stride] = jnp.where(keep, pltpu.roll(low, 128 - stride * width, 1), high)
-        stride *= 2
+                blocks[at] = jnp.where(keep, low, pltpu.roll(high, width, 1))
+                blocks[at | stride] = jnp.where(keep, pltpu.roll(low, 128 - width, 1), high)
     return blocks
 
 
 def layer_norm(values):
-    centred = values - jnp.mean(values, axis=0, keepdims=True)
-    inverse = lax.rsqrt(jnp.mean(centred * centred, axis=0, keepdims=True) + EPSILON)
+    centred = values - jnp.mean(values, axis=1, keepdims=True)
+    inverse = lax.rsqrt(jnp.mean(centred * centred, axis=1, keepdims=True) + EPSILON)
     return (centred * inverse, inverse)
 
 
 def norm_back(normed, inverse, upstream):
     return inverse * (
         upstream
-        - jnp.mean(upstream, axis=0, keepdims=True)
-        - normed * jnp.mean(upstream * normed, axis=0, keepdims=True)
+        - jnp.mean(upstream, axis=1, keepdims=True)
+        - normed * jnp.mean(upstream * normed, axis=1, keepdims=True)
     )
-
-
-def near_of(group):
-    return ((group // 4) * 2 + group % 2, (group // 2) % 2)
 
 
 def body(
@@ -133,9 +130,9 @@
     trig_hbm,
     phase_hbm,
     quad_hbm,
-    out_hbm,
-    gx_hbm,
-    gf_hbm,
+    out_ref,
+    gx_ref,
+    gf_ref,
     send_near,
     recv_near,
     send_far,
@@ -152,12 +149,10 @@
     leg_out,
     trig_v,
     trig_down,
-    trig_wide,
+    trig_up,
     phase_v,
     taps_v,
-    xt_v,
     normed_v,
-    cott_v,
     dhid_v,
     wint_v,
     woutt_v,
@@ -170,11 +165,7 @@
     ext_ref,
     filt_ref,
     quad_ref,
-    out_ref,
-    gx_ref,
-    gf_ref,
     load_sem,
-    store_sem,
     ring_sem,
     send_sem,
     recv_sem,
@@ -185,6 +176,50 @@
     near_me = x_at * 2 + core
     far_me = half * LATS + lat
     z_me, y_me = (far_me // 8, lax.rem(far_me, 8))
+
+    def over_near(action):
+        for move in NEAREST:
+            peer = lax.rem(near_me + move, NEAR)
+            action(peer, (lat, (peer // 2) * 4 + half * 2 + lax.rem(peer, 2)))
+
+    def loop(count, action):
+        def run(step, carry):
+            action(step)
+            return carry
+
+        lax.fori_loop(0, count, run, 0)
+
+    far_y = [lax.rem(y_me + move, 8) for move in FARTHEST]
+
+    def far_device(peer_z, peer_y):
+        peer_lat = lax.rem(peer_z, 4) * 8 + peer_y
+        peer_lon = x_at * 4 + (peer_z // 4) * 2 + core
+        return (peer_z * 8 + peer_y, peer_lat, (peer_lat, peer_lon))
+
+    def over_far(action):
+        def plane(step):
+            away = (step + 1) // 2
+            peer_z = lax.rem(z_me + 4 + away * (1 - 2 * lax.rem(step, 2)), 8)
+            for peer_y in far_y:
+                action(*far_device(peer_z, peer_y))
+
+        loop(7, plane)
+        for peer_y in far_y[:-1]:
+            action(*far_device(z_me, peer_y))
+
+    def ring_z(move):
+        return far_device(lax.rem(z_me + move, 8), y_me)[2]
+
+    barrier = pltpu.get_barrier_semaphore()
+
+    def greet(device):
+        pl.semaphore_signal(barrier, inc=1, device_id=device, device_id_type=MESH)
+
+    over_near(lambda peer, device: greet(device))
+    for move in FARTHEST[:-1]:
+        greet(ring_z(move))
+    for peer_y in far_y[:-1]:
+        greet(far_device(z_me, peer_y)[2])
 
     loads = []
     for index, (source, target) in enumerate(
@@ -207,53 +242,8 @@
         copy.start()
         loads.append(copy)
 
-    def near_peer(step):
-        step = step + (step >= 4).astype(jnp.int32)
-        peer = lax.rem(near_me + 4 + step, NEAR)
-        return (peer, (lat, (peer // 2) * 4 + half * 2 + lax.rem(peer, 2)))
-
-    def loop(count, action):
-        def run(step, carry):
-            action(step)
-            return carry
-
-        lax.fori_loop(0, count, run, 0)
-
-    far_y = [lax.rem(y_me + move, 8) for move in FARTHEST]
-
-    def far_device(peer_z, peer_y):
-        peer_lat = lax.rem(peer_z, 4) * 8 + peer_y
-        peer_lon = x_at * 4 + (peer_z // 4) * 2 + core
-        return (peer_z * 8 + peer_y, peer_lat, (peer_lat, peer_lon))
-
-    def over_far(action):
-        def plane(step):
-            away = (step + 1) // 2
-            peer_z = lax.rem(z_me + 4 + away * (1 - 2 * lax.rem(step, 2)), 8)
-            for peer_y in far_y:
-                action(*far_device(peer_z, peer_y))
-
-        loop(7, plane)
-        for peer_y in far_y[:-1]:
-            action(*far_device(z_me, peer_y))
-
-    def ring_z(move):
-        return far_device(lax.rem(z_me + move, 8), y_me)[2]
-
-    barrier = pltpu.get_barrier_semaphore()
-
-    def greet(device):
-        pl.semaphore_signal(barrier, inc=1, device_id=device, device_id_type=MESH)
-
-    for move in FARTHEST[:-1]:
-        greet(ring_z(move))
-    for peer_y in far_y[:-1]:
-        greet(far_device(z_me, peer_y)[2])
-    loop(NEAR - 1, lambda step: greet(near_peer(step)[1]))
-
     def start_near(at):
-        def action(step):
-            peer, device = near_peer(step)
+        def action(peer, device):
             pltpu.make_async_remote_copy(
                 src_ref=send_near.at[at, peer],
                 dst_ref=recv_near.at[at, near_me],
@@ -263,7 +253,7 @@
                 device_id_type=MESH,
             ).start()
 
-        loop(NEAR - 1, action)
+        over_near(action)
         recv_near[at, near_me] = send_near[at, near_me]
 
     def wait_near(at):
@@ -288,67 +278,64 @@
         block = recv_far.at[at, pl.ds(0, FAR - 1)]
         pltpu.make_async_copy(block, block, recv_sem.at[4 + at]).wait()
 
-    def send_field(at, field):
-        for group in range(CHANS // GROUP):
-            near, part = near_of(group)
-            send_near[at, near, part * GROUP : (part + 1) * GROUP, :] = field[
-                group * GROUP : (group + 1) * GROUP
-            ].astype(BF16)
-        start_near(at)
-
-    def take_field(at):
-        pieces = []
-        for group in range(CHANS // GROUP):
-            near, part = near_of(group)
-            pieces.append(recv_near[at, near, part * GROUP : (part + 1) * GROUP, :].astype(F32))
-        return jnp.concatenate(pieces, axis=0)
-
-    def to_spectrum(near_at, far_at):
-        rows = [recv_near[near_at, near].astype(F32) for near in range(NEAR)]
-        first = swap_blocks(rows[:4], COLS)
-        second = swap_blocks(rows[4:], COLS)
-        field = jnp.concatenate(
-            [jnp.concatenate([first[a], second[a]], axis=1) for a in range(ROWS)], axis=0
-        ).astype(BF16)
-        parts = mm(trig_down[...], field, 1, 1)
-        parts = parts[0 : PARTS * LATS] + parts[PARTS * LATS :]
-        blocks = swap_blocks([parts[at * LATS : (at + 1) * LATS] for at in range(PARTS)], GROUP)
-        flat = send_far.at[far_at].reshape(FAR * ROWS, 128)
-        for a in range(ROWS):
-            for part in range(2):
-                flat[pl.ds(part * LATS * ROWS + a, LATS, stride=ROWS), :] = blocks[a * 2 + part]
-        if far_at == 0:
-            pl.semaphore_wait(ring_sem, 7)
-        start_far(far_at, False)
-
-    def take_spectrum(far_at):
-        flat = recv_far.at[far_at].reshape(FAR * ROWS, 128)
-        return (flat[0:NLAT, :] + flat[NLAT : 2 * NLAT, :]).T
-
-    def send_spectrum(far_at, field):
-        flat = send_far.at[far_at].reshape(FAR * ROWS, 128)
-        flat[0:NLAT, :] = field.T
-        start_far(far_at, True)
-
-    def to_grid(far_at, near_at):
-        flat = recv_far.at[far_at].reshape(FAR * ROWS, 128)
-        rows = []
-        for a in range(ROWS):
-            for part in range(2):
-                rows.append(flat[pl.ds(part * LATS * ROWS + a, LATS, stride=ROWS), :])
-        stacked = jnp.concatenate(swap_blocks(rows, GROUP), axis=0).astype(BF16)
-        field = mm(stacked, trig_wide[...], 0, 0)
-        field = field[:, 0 : NEAR * COLS] + field[:, NEAR * COLS :]
+    def fill_field(at, field):
         for side in range(2):
             blocks = swap_blocks(
                 [
                     field[a * COLS : (a + 1) * COLS, side * 128 : (side + 1) * 128]
                     for a in range(ROWS)
                 ],
-                COLS,
+                FIELD_STEPS,
             )
-            for at in range(4):
-                send_near[near_at, side * 4 + at] = blocks[at].astype(BF16)
+            for near in range(4):
+                send_near[at, side * 4 + near] = blocks[near].astype(BF16)
+
+    def take_field(at):
+        sides = [
+            jnp.concatenate(
+                swap_blocks(
+                    [recv_near[at, side * 4 + near].astype(F32) for near in range(4)], FIELD_STEPS
+                ),
+                axis=0,
+            )
+            for side in range(2)
+        ]
+        return jnp.concatenate(sides, axis=1)
+
+    def spectrum_rows(flat, spot):
+        row, part = (2 * (spot // 4) + spot % 2, spot // 2 % 2)
+        return flat.at[pl.ds(part * LATS * ROWS + row, LATS, stride=ROWS), :]
+
+    def to_spectrum(near_at, far_at):
+        field = recv_near[near_at].reshape(NEAR * COLS, 128)
+        parts = mm(trig_down[...], field)
+        parts = parts[0 : PARTS * LATS] + parts[PARTS * LATS :]
+        blocks = swap_blocks(
+            [parts[at * LATS : (at + 1) * LATS] for at in range(PARTS)], ORDER_STEPS
+        )
+        flat = send_far.at[far_at].reshape(FAR * ROWS, 128)
+        for spot in range(PARTS):
+            spectrum_rows(flat, spot)[...] = blocks[spot]
+        if far_at == 0:
+            pl.semaphore_wait(ring_sem, 7)
+        start_far(far_at, False)
+
+    def take_spectrum(far_at):
+        flat = recv_far.at[far_at].reshape(FAR * ROWS, 128)
+        return (flat[0:NLAT, :] + flat[NLAT : 2 * NLAT, :]).T
+
+    def send_spectrum(far_at, field):
+        flat = send_far.at[far_at].reshape(FAR * ROWS, 128)
+        flat[0:NLAT, :] = field.T
+        start_far(far_at, True)
+
+    def to_grid(far_at, near_at):
+        flat = recv_far.at[far_at].reshape(FAR * ROWS, 128)
+        rows = [spectrum_rows(flat, spot)[...] for spot in range(PARTS)]
+        stacked = jnp.concatenate(swap_blocks(rows, ORDER_STEPS), axis=0).astype(BF16)
+        field = mm(trig_up[...], stacked)
+        field = (field[0 : NEAR * COLS] + field[NEAR * COLS :]).astype(BF16)
+        send_near[near_at] = field.reshape(NEAR, COLS, 128)
         start_near(near_at)
 
     def analyse(rows, at):
@@ -363,12 +350,11 @@
         return jnp.where(lat * ORDERS + at == 0, 1.0, 2.0).astype(F32)
 
     loads[0].wait()
-    xt = x_ref[...].astype(F32).T
-    normed, inverse_in = layer_norm(xt)
-    xt_v[...] = xt
+    normed, inverse_in = layer_norm(x_ref[...].astype(F32))
     normed_v[...] = normed
+    fill_field(0, normed)
     pl.semaphore_wait(barrier, NEAR - 1 + 7 + 7)
-    send_field(0, normed)
+    start_near(0)
     for move in FARTHEST[:-1]:
         pl.semaphore_signal(ring_sem, inc=1, device_id=ring_z(move), device_id_type=MESH)
 
@@ -377,8 +363,9 @@
     high, low = split(trig_v[...])
     trig_down[0 : PARTS * LATS] = high
     trig_down[PARTS * LATS :] = low
-    trig_wide[:, 0 : NEAR * COLS] = high
-    trig_wide[:, NEAR * COLS :] = low
+    high, low = split(trig_v[...].T)
+    trig_up[0 : NEAR * COLS] = high
+    trig_up[NEAR * COLS :] = low
     lat_at = lax.broadcasted_iota(jnp.int32, (TAPS, 128), 1)
     shift = lax.broadcasted_iota(jnp.int32, (TAPS, 128), 0) - REACH
     for r in range(TAPS):
@@ -405,11 +392,9 @@
         leg_in[at, :, 0:NLAT] = high
         leg_in[at, :, NLAT:] = low
     mix = mix_v[...].reshape(BASIS * GROUP, GROUP)
-    cott = cot_ref[...].astype(F32).T
-    cott_v[...] = cott
-    dhid_v[...] = mm(wout_v[...], cott.astype(BF16))
     wint_v[...] = win_v[...].T
     woutt_v[...] = wout_v[...].T
+    dhid_v[...] = mm(cot_ref[...], woutt_v[...])
     quad = quad_ref[0:1, :]
     filter_real, filter_imag = (filt_ref[0], filt_ref[1])
 
@@ -455,21 +440,19 @@
     to_grid(1, 1)
     wait_near(1)
 
-    carried = xt_v[...] + take_field(1)
+    carried = x_ref[...].astype(F32) + take_field(1)
     normed_mid, inverse_mid = layer_norm(carried)
-    preact = mm(wint_v[...], normed_mid.astype(BF16))
+    preact = mm(normed_mid.astype(BF16), win_v[...])
     bell = jnp.exp(-0.5 * preact * preact) * (1.0 / math.sqrt(2.0 * math.pi))
     gate = 0.5 * (1.0 + lax.erf(preact * (1.0 / math.sqrt(2.0))))
     d_preact = (dhid_v[...] * (gate + preact * bell)).astype(BF16)
-    d_normed = mm(win_v[...], d_preact)
-    d_carried = cott_v[...] + norm_back(normed_mid, inverse_mid, d_normed)
-    send_field(2, d_carried)
+    d_normed = mm(d_preact, wint_v[...])
+    d_carried = cot_ref[...].astype(F32) + norm_back(normed_mid, inverse_mid, d_normed)
+    fill_field(2, d_carried)
+    start_near(2)
     dcar_v[...] = d_carried
     hidden = (preact * gate).astype(BF16)
-    output = carried + mm(woutt_v[...], hidden)
-    out_ref[...] = output.T.astype(BF16)
-    store_out = pltpu.make_async_copy(out_ref, out_hbm, store_sem.at[0])
-    store_out.start()
+    out_ref[...] = (carried + mm(hidden, wout_v[...])).astype(BF16)
 
     wait_near(2)
     to_spectrum(2, 2)
@@ -516,7 +499,8 @@
             device_id_type=MESH,
         ).start()
 
-    loop(LATS - 1, scatter)
+    for step in range(LATS - 1):
+        scatter(step)
     grad_recv[lat] = grad_send[lat]
 
     pieces = []
@@ -560,15 +544,11 @@
     wait_near(3)
     d_normed_in = take_field(3)
     grad_x = dcar_v[...] + norm_back(normed_v[...], inverse_in, d_normed_in)
-    gx_ref[...] = grad_x.T.astype(BF16)
-    store_gx = pltpu.make_async_copy(gx_ref, gx_hbm, store_sem.at[1])
-    store_gx.start()
+    gx_ref[...] = grad_x.astype(BF16)
 
     block = grad_all.at[pl.ds(0, LATS - 1)]
     pltpu.make_async_copy(block, block, recv_sem.at[9]).wait()
     gf_ref[...] = grad_all.reshape(2 * GROUP, 128)[...]
-    store_gf = pltpu.make_async_copy(gf_ref, gf_hbm, store_sem.at[2])
-    store_gf.start()
 
     for at in range(4):
         block = send_near.at[at, pl.ds(0, NEAR - 1)]
@@ -578,9 +558,6 @@
     block = grad_send.at[pl.ds(0, LATS - 1)]
     pltpu.make_async_copy(block, block, send_sem.at[8]).wait()
     pltpu.make_async_copy(block, block, send_sem.at[9]).wait()
-    store_out.wait()
-    store_gx.wait()
-    store_gf.wait()
 
 
 def hand_out(first, second, third, first_out, second_out, third_out):
@@ -596,12 +573,12 @@
     out, grad_x, grad_filter = pl.pallas_call(
         body,
         out_shape=(
-            jax.ShapeDtypeStruct((cells, CHANS), BF16),
-            jax.ShapeDtypeStruct((cells, CHANS), BF16),
-            jax.ShapeDtypeStruct((2 * GROUP, 128), F32),
+            pltpu.VMEM((cells, CHANS), BF16),
+            pltpu.VMEM((cells, CHANS), BF16),
+            pltpu.VMEM((2 * GROUP, 128), F32),
         ),
         in_specs=[hbm] * 12,
-        out_specs=(hbm, hbm, hbm),
+        out_specs=(vmem, vmem, vmem),
         scratch_shapes=[
             pltpu.VMEM((4, NEAR, 2 * GROUP, 128), BF16),
             pltpu.VMEM((4, NEAR, 2 * GROUP, 128), BF16),
@@ -619,29 +596,23 @@
             pltpu.VMEM((ORDERS, NLAT, 2 * NLAT), BF16),
             pltpu.VMEM((PARTS * LATS, NEAR * COLS), F32),
             pltpu.VMEM((2 * PARTS * LATS, NEAR * COLS), BF16),
-            pltpu.VMEM((PARTS * LATS, 2 * NEAR * COLS), BF16),
+            pltpu.VMEM((2 * NEAR * COLS, PARTS * LATS), BF16),
             pltpu.VMEM((TAPS, PARTS, 128), F32),
             pltpu.VMEM((BASIS, TAPS, PARTS, 128), F32),
-            pltpu.VMEM((CHANS, cells), F32),
-            pltpu.VMEM((CHANS, cells), F32),
-            pltpu.VMEM((CHANS, cells), F32),
-            pltpu.VMEM((HIDDEN, cells), F32),
+            pltpu.VMEM((cells, CHANS), F32),
+            pltpu.VMEM((cells, HIDDEN), F32),
             pltpu.VMEM((HIDDEN, CHANS), BF16),
             pltpu.VMEM((CHANS, HIDDEN), BF16),
             pltpu.VMEM((BASIS * GROUP, 2 * ORDERS * 128), BF16),
             pltpu.VMEM((ORDERS, 2 * GROUP, 128), F32),
-            pltpu.VMEM((CHANS, cells), F32),
+            pltpu.VMEM((cells, CHANS), F32),
             pltpu.VMEM((cells, CHANS), BF16),
             pltpu.VMEM((cells, CHANS), BF16),
             pltpu.VMEM((BASIS, TAPS, TAPS, NLAT), BF16),
             pltpu.VMEM((TAPS, 2, NLAT), jnp.int32),
             pltpu.VMEM((2, GROUP, NLAT), F32),
             pltpu.VMEM((8, NLAT), F32),
-            pltpu.VMEM((cells, CHANS), BF16),
-            pltpu.VMEM((cells, CHANS), BF16),
-            pltpu.VMEM((2 * GROUP, 128), F32),
             pltpu.SemaphoreType.DMA((12,)),
-            pltpu.SemaphoreType.DMA((3,)),
             pltpu.SemaphoreType.REGULAR,
             pltpu.SemaphoreType.DMA((10,)),
             pltpu.SemaphoreType.DMA((10,)),
@@ -664,6 +635,9 @@
         phase_values(),
         quad_values(),
     )
+    out, grad_x, grad_filter = (
+        pltpu.with_memory_space_constraint(value, pltpu.VMEM) for value in (out, grad_x, grad_filter)
+    )
     out, grad_x, grad_filter = pl.pallas_call(
         hand_out,
         out_shape=(

time: 67.9 us -> 65.8 us (0.969)
  Pallas kernels: 67.1 us -> 65 us
    pallas_call x1, Pallas kernels: 65.6 us -> 64.4 us  [local(): pl.pallas_call(body, out_shape=(pltpu.VMEM((cells, CHANS), BF16), pltpu.V...]
    pallas_call x1, Pallas kernels: 1.53 us -> 0.66 us  [local(): pl.pallas_call(hand_out, out_shape=(jax.ShapeDtypeStruct((cells, CHANS),...]
where the time goes in v4:
time: 65.8 us; the launch traced here: 65.7 us
  Pallas kernels  65 us (99%)
    pallas_call x1, Pallas kernels, local(): pl.pallas_call(body, out_shape=(pltpu.VMEM((cells, CHANS), BF16), pltpu.V...  64.4 us

profile of v4, /device:TPU:1, one launch (start us, length us, event | category | flops | bytes accessed | tf_op | source)
XLA Modules:
  0.0 65.7 jit_solution(6925461055301919144)
XLA Ops:
  0.6 64.4 %block.1 = (bf16[128,256]{1,0:T(8,128)(2,1)S(1)}, bf16[128,256]{1,0:T(8,128)(2,1)S(1)}, f32[32,128]{1,0:T(8,128)S(1)}) custom-call(bf16[128,256]{1,0:T(8,128)(2,1)} %bitcast.8, bf16[128,256]{1,0:T(8,128)(2,1)} %bitcast.9, bf16[9,7,7,128]{3,2,1,0:T(8,128)(2,1)} %bitcast.7, s32[7,2,128]{2,1,0:T(2,128)} %bitcast.10, f32[2,16,128]{2,1,0:T(8,128)} %filt_hbm.1, ...), custom_call_target="tpu_custom_call" | custom-call | tf_op jit(solution)/shard_map/block/pallas_call | solution.py:573
  65.0 0.7 %hand_out.1 = (bf16[128,256]{1,0:T(8,128)(2,1)}, bf16[128,256]{1,0:T(8,128)(2,1)}, f32[32,128]{1,0:T(8,128)}) custom-call(bf16[128,256]{1,0:T(8,128)(2,1)S(1)} %get-tuple-element.9.first, bf16[128,256]{1,0:T(8,128)(2,1)S(1)} %get-tuple-element.10.second, f32[32,128]{1,0:T(8,128)S(1)} %get-tuple-element.11.third), custom_call_target="tpu_custom_call" | custom-call | tf_op jit(solution)/shard_map/hand_out/pallas_call | solution.py:641

commit v5 on v4

--- a/solution.py
+++ b/solution.py
@@ -83,11 +83,6 @@
     return lax.dot_general(
         left, right, (((left_dim,), (right_dim,)), ((), ())), preferred_element_type=F32
     )
-
-
-def split(values):
-    high = values.astype(BF16)
-    return (high, (values - high.astype(F32)).astype(BF16))
 
 
 def swap_blocks(blocks, steps):
@@ -282,25 +277,25 @@
         for side in range(2):
             blocks = swap_blocks(
                 [
-                    field[a * COLS : (a + 1) * COLS, side * 128 : (side + 1) * 128]
+                    field[a * COLS : (a + 1) * COLS, side * 128 : (side + 1) * 128].astype(BF16)
                     for a in range(ROWS)
                 ],
                 FIELD_STEPS,
             )
             for near in range(4):
-                send_near[at, side * 4 + near] = blocks[near].astype(BF16)
+                send_near[at, side * 4 + near] = blocks[near]
 
     def take_field(at):
         sides = [
             jnp.concatenate(
                 swap_blocks(
-                    [recv_near[at, side * 4 + near].astype(F32) for near in range(4)], FIELD_STEPS
+                    [recv_near[at, side * 4 + near] for near in range(4)], FIELD_STEPS
                 ),
                 axis=0,
             )
             for side in range(2)
         ]
-        return jnp.concatenate(sides, axis=1)
+        return jnp.concatenate(sides, axis=1).astype(F32)
 
     def spectrum_rows(flat, spot):
         row, part = (2 * (spot // 4) + spot % 2, spot // 2 % 2)
@@ -309,7 +304,6 @@
     def to_spectrum(near_at, far_at):
         field = recv_near[near_at].reshape(NEAR * COLS, 128)
         parts = mm(trig_down[...], field)
-        parts = parts[0 : PARTS * LATS] + parts[PARTS * LATS :]
         blocks = swap_blocks(
             [parts[at * LATS : (at + 1) * LATS] for at in range(PARTS)], ORDER_STEPS
         )
@@ -331,20 +325,17 @@
 
     def to_grid(far_at, near_at):
         flat = recv_far.at[far_at].reshape(FAR * ROWS, 128)
-        rows = [spectrum_rows(flat, spot)[...] for spot in range(PARTS)]
-        stacked = jnp.concatenate(swap_blocks(rows, ORDER_STEPS), axis=0).astype(BF16)
+        rows = [spectrum_rows(flat, spot)[...].astype(BF16) for spot in range(PARTS)]
+        stacked = jnp.concatenate(swap_blocks(rows, ORDER_STEPS), axis=0)
         field = mm(trig_up[...], stacked)
-        field = (field[0 : NEAR * COLS] + field[NEAR * COLS :]).astype(BF16)
-        send_near[near_at] = field.reshape(NEAR, COLS, 128)
+        send_near[near_at] = field.astype(BF16).reshape(NEAR, COLS, 128)
         start_near(near_at)
 
     def analyse(rows, at):
-        both = mm(rows.astype(BF16), leg_in[at])
-        return both[:, 0:NLAT] + both[:, NLAT:]
+        return mm(rows.astype(BF16), leg_in[at])
 
     def synthesise(rows, at):
-        both = mm(rows.astype(BF16), leg_out[at])
-        return both[:, 0:NLAT] + both[:, NLAT:]
+        return mm(rows.astype(BF16), leg_out[at])
 
     def order_weight(at):
         return jnp.where(lat * ORDERS + at == 0, 1.0, 2.0).astype(F32)
@@ -360,12 +351,8 @@
 
     for copy in loads[1:5]:
         copy.wait()
-    high, low = split(trig_v[...])
-    trig_down[0 : PARTS * LATS] = high
-    trig_down[PARTS * LATS :] = low
-    high, low = split(trig_v[...].T)
-    trig_up[0 : NEAR * COLS] = high
-    trig_up[NEAR * COLS :] = low
+    trig_down[...] = trig_v[...].astype(BF16)
+    trig_up[...] = trig_v[...].T.astype(BF16)
     lat_at = lax.broadcasted_iota(jnp.int32, (TAPS, 128), 1)
     shift = lax.broadcasted_iota(jnp.int32, (TAPS, 128), 0) - REACH
     for r in range(TAPS):
@@ -385,12 +372,8 @@
     to_spectrum(0, 0)
 
     for at in range(ORDERS):
-        high, low = split(leg_v[at])
-        leg_out[at, :, 0:NLAT] = high
-        leg_out[at, :, NLAT:] = low
-        high, low = split(leg_v[at].T)
-        leg_in[at, :, 0:NLAT] = high
-        leg_in[at, :, NLAT:] = low
+        leg_out[at] = leg_v[at].astype(BF16)
+        leg_in[at] = leg_v[at].T.astype(BF16)
     mix = mix_v[...].reshape(BASIS * GROUP, GROUP)
     wint_v[...] = win_v[...].T
     woutt_v[...] = wout_v[...].T
@@ -592,11 +575,11 @@
             pltpu.VMEM((CHANS, HIDDEN), BF16),
             pltpu.VMEM((HIDDEN, CHANS), BF16),
             pltpu.VMEM((ORDERS, NLAT, NLAT), F32),
-            pltpu.VMEM((ORDERS, NLAT, 2 * NLAT), BF16),
-            pltpu.VMEM((ORDERS, NLAT, 2 * NLAT), BF16),
+            pltpu.VMEM((ORDERS, NLAT, NLAT), BF16),
+            pltpu.VMEM((ORDERS, NLAT, NLAT), BF16),
             pltpu.VMEM((PARTS * LATS, NEAR * COLS), F32),
-            pltpu.VMEM((2 * PARTS * LATS, NEAR * COLS), BF16),
-            pltpu.VMEM((2 * NEAR * COLS, PARTS * LATS), BF16),
+            pltpu.VMEM((PARTS * LATS, NEAR * COLS), BF16),
+            pltpu.VMEM((NEAR * COLS, PARTS * LATS), BF16),
             pltpu.VMEM((TAPS, PARTS, 128), F32),
             pltpu.VMEM((BASIS, TAPS, PARTS, 128), F32),
             pltpu.VMEM((cells, CHANS), F32),

time: 65.8 us -> 65.5 us (level)
  no operation moved by 1% of the time
where the time goes in v5:
time: 65.5 us; the launch traced here: 65.3 us
  Pallas kernels  64.7 us (99%)
    pallas_call x1, Pallas kernels, local(): pl.pallas_call(body, out_shape=(pltpu.VMEM((cells, CHANS), BF16), pltpu.V...  64 us

profile of v5, /device:TPU:1, one launch (start us, length us, event | category | flops | bytes accessed | tf_op | source)
XLA Modules:
  0.0 65.3 jit_solution(17235678555002408246)
XLA Ops:
  0.6 64.0 %block.1 = (bf16[128,256]{1,0:T(8,128)(2,1)S(1)}, bf16[128,256]{1,0:T(8,128)(2,1)S(1)}, f32[32,128]{1,0:T(8,128)S(1)}) custom-call(bf16[128,256]{1,0:T(8,128)(2,1)} %bitcast.8, bf16[128,256]{1,0:T(8,128)(2,1)} %bitcast.9, bf16[9,7,7,128]{3,2,1,0:T(8,128)(2,1)} %bitcast.7, s32[7,2,128]{2,1,0:T(2,128)} %bitcast.10, f32[2,16,128]{2,1,0:T(8,128)} %filt_hbm.1, ...), custom_call_target="tpu_custom_call" | custom-call | tf_op jit(solution)/shard_map/block/pallas_call | solution.py:556
  64.7 0.7 %hand_out.1 = (bf16[128,256]{1,0:T(8,128)(2,1)}, bf16[128,256]{1,0:T(8,128)(2,1)}, f32[32,128]{1,0:T(8,128)}) custom-call(bf16[128,256]{1,0:T(8,128)(2,1)S(1)} %get-tuple-element.9.first, bf16[128,256]{1,0:T(8,128)(2,1)S(1)} %get-tuple-element.10.second, f32[32,128]{1,0:T(8,128)S(1)} %get-tuple-element.11.third), custom_call_target="tpu_custom_call" | custom-call | tf_op jit(solution)/shard_map/hand_out/pallas_call | solution.py:624
